TPU v7x, 32 devices: a whole 2x2x4 slice. The times are simulated.
32 devices in a mesh: row: 4 (over y, core), col: 8 (over z, x).
Axes of the slice: x: 2, y: 2, z: 4, core: 2. Of those that a mesh axis runs over, the one named last changes fastest.
Arguments:
- matrix: float32 [4096, 4096], P('row', 'col'), may hold values from -4 to 4, as said below
- panel: float32 [4096, 64], P('row'), may hold values from -1200 to 1200
Outputs:
- updated: float32 [4096, 4096], P('row', 'col')
- w_rows: float32 [4096, 64], P('row')
- basis: float32 [4096, 64], P('row')
Inputs may be any that keep to these rules, and one draw needn't show every extreme that they name: Read in global order (both indices mapped back through their cyclic orders) the matrix is exactly symmetric.
All inputs are finite; a program needn't handle non-finite values.
Results may differ from a plain program's by a relative error of at most 0.00007.
Values sent between devices are 32-bit elements; how exact they have to be, the bound alone decides.
No kernel may reach another device: no remote copies, remote signals or barrier semaphores. Data moves between devices by JAX's collectives and lax.ppermute only.
A program may use at most 64 MiB of HBM per device.

v0:
```python
import functools

import jax
import jax.numpy as jnp
from jax import lax
from jax.experimental import pallas as pl
from jax.experimental.pallas import tpu as pltpu
from jax.sharding import PartitionSpec as P

HIGH = lax.Precision.HIGHEST
VMEM = pl.BlockSpec(memory_space=pltpu.VMEM)
SMEM = pl.BlockSpec(memory_space=pltpu.SMEM)
HBM = pl.BlockSpec(memory_space=pltpu.HBM)
PARAMS = pltpu.CompilerParams(vmem_limit_bytes=40 * 1024 * 1024)
STRIP = 8


def dot(left, right, contract, precision=HIGH):
    return lax.dot_general(
        left, right, (contract, ((), ())), precision=precision, preferred_element_type=jnp.float32
    )


def dot16(left, right, contract):
    return dot(left, right, contract, lax.Precision.DEFAULT)


def split(value, parts):
    terms = []
    for _ in range(parts):
        terms.append(value.astype(jnp.bfloat16))
        value = value - terms[-1].astype(jnp.float32)
    return terms


def partner(value, axis, step):
    size = lax.axis_size(axis)
    return lax.ppermute(value, axis, [(i, i ^ step) for i in range(size)])


def spread_rows(value, after):
    n_row, n_col = lax.axis_size("row"), lax.axis_size("col")
    apart = lax.axis_index("row") ^ (lax.axis_index("col") % n_row)
    bits = [1] + [1 << i for i in reversed(range(1, n_row.bit_length() - 1))]
    reached = [0]
    for bit in bits:
        pairs = []
        for c in range(n_col):
            for offset in reached:
                source = (c % n_row) ^ offset
                pairs.append((source * n_col + c, (source ^ bit) * n_col + c))
        reached += [offset ^ bit for offset in reached]
        received = lax.ppermute(value, ("row", "col"), pairs)
        takes = apart & bit != 0
        if bit == bits[-1]:
            return value, received, takes.astype(jnp.int32).reshape(1)
        received, _ = lax.optimization_barrier((received, after))
        value = jnp.where(takes, received, value)


def transpose_grid(value, shift):
    n_row, n_col = lax.axis_size("row"), lax.axis_size("col")
    ratio = n_col // n_row
    pairs = []
    for r in range(n_row):
        for k in range(ratio):
            for q in range(n_row):
                column = (k + shift) % ratio * n_row + r
                row = q if shift % 2 else q ^ (n_row // 2)
                pairs.append((row * n_col + column, r * n_col + k * n_row + q))
    return lax.ppermute(value, ("row", "col"), pairs)


def copy_rows(source, target, sems, first, pieces):
    size = source.shape[0] // pieces
    copies = []
    for piece in range(pieces):
        span = slice(piece * size, (piece + 1) * size)
        copies.append(
            pltpu.make_async_copy(source.at[span, :], target.at[span, :], sems.at[first + piece])
        )
        copies[-1].start()
    return copies


def panel_kernel(
    ratio, which_ref, panel_ref, matrix_ref,
    mine_ref, held_ref, terms_ref, gram_ref, kept_ref, sems,
):
    width = panel_ref.shape[0]
    pieces = sems.shape[0] // 2
    panel_copies = copy_rows(panel_ref, held_ref, sems, 0, pieces)
    matrix_copies = copy_rows(matrix_ref, kept_ref, sems, pieces, pieces)
    for copy in panel_copies:
        copy.wait()
    which = which_ref[0]
    for j in range(mine_ref.shape[1] // width):
        start = j * ratio * width
        block = held_ref[:, start : start + width]
        for k in range(1, ratio):
            start += width
            block = jnp.where(which == k, held_ref[:, start : start + width], block)
        mine_ref[:, j * width : (j + 1) * width] = block
    panel = held_ref[...]
    terms_ref[...] = jnp.concatenate(split(panel, 3), axis=0)
    to_strip(dot(panel, panel, ((1,), (1,))), gram_ref)
    for copy in matrix_copies:
        copy.wait()


def product_kernel(terms_ref, matrix_ref, gram_ref, out_ref):
    width = out_ref.shape[0] - STRIP
    rows = matrix_ref.shape[0]
    chunk = 256
    total = jnp.zeros((width, matrix_ref.shape[1]), jnp.float32)
    for start in range(0, rows, chunk):
        span = slice(start, start + chunk)
        parts = split(matrix_ref[span, :], 3)
        for i, part in enumerate(parts):
            count = 3 - i
            out = dot16(terms_ref[: count * width, span], part, ((1,), (0,)))
            for t in range(count):
                total = total + out[t * width : (t + 1) * width, :]
    out_ref[:width, :] = total
    out_ref[width:, :] = gram_ref[...]


def to_strip(value, strip_ref):
    width = value.shape[0]
    for i in range(width // STRIP):
        strip_ref[:, i * width : (i + 1) * width] = value[i * STRIP : (i + 1) * STRIP, :]


def from_strip(strip, width):
    return jnp.concatenate(
        [strip[:, i * width : (i + 1) * width] for i in range(width // STRIP)], axis=0
    )


def finish_kernel(other_ref, mine_ref, product_ref, gram_ref):
    width = product_ref.shape[0]
    product_ref[...] = mine_ref[:width, :] + other_ref[:width, :]
    gram_ref[...] = from_strip(mine_ref[width:, :] + other_ref[width:, :], width)


def factor_kernel(gram_ref, inverse_ref):
    size = inverse_ref.shape[0]
    batch = 4
    row = lax.broadcasted_iota(jnp.int32, (size, 2 * size), 0)
    lane = lax.broadcasted_iota(jnp.int32, (size, 2 * size), 1)
    eye = jnp.where(row == lane, 1.0, 0.0).astype(jnp.float32)
    table = jnp.concatenate([eye[:, :size], gram_ref[...]], axis=1)
    for first in range(0, size, batch):
        base = first // 8 * 8
        height = size - base
        low = table[base:, :]
        low_row = row[base:, :]
        cols = [
            jnp.broadcast_to(low[:, size + first + t : size + first + t + 1], (height, 2 * size))
            for t in range(batch)
        ]
        rows = [low[first - base + t : first - base + t + 1, :] for t in range(batch)]
        for t in range(batch):
            at = first - base + t
            scale = 1.0 / cols[t][at : at + 1, :]
            factor = jnp.where(low_row > first + t, cols[t] * scale, 0.0)
            for s in range(t + 1, batch):
                cols[s] = cols[s] - factor * cols[s][at : at + 1, :]
                rows[s] = rows[s] - factor[first - base + s : first - base + s + 1, :] * rows[t]
            low = low - factor * rows[t]
        table = low if base == 0 else jnp.concatenate([table[:base, :], low], axis=0)
    diagonal = jnp.sum(jnp.where(lane == row + size, table, 0.0), axis=1, keepdims=True)
    inverse_ref[...] = (table / jnp.sqrt(diagonal))[:, :size]


def stack_left(value):
    high, low = split(value, 2)
    return jnp.concatenate([high, low, high], axis=0)


def stack_right(value):
    high, low = split(value, 2)
    return jnp.concatenate([high, high, low], axis=0)


def basis_kernel(
    matrix_ref, panel_ref, product_cols_ref, inverse_ref, received_ref, held_ref, takes_ref,
    begun_ref, basis_ref, kept_ref, cols_ref,
):
    inverse = inverse_ref[...]
    basis = dot(inverse, panel_ref[...], ((1,), (0,)))
    image_cols = dot(inverse, product_cols_ref[...], ((1,), (0,)))
    basis_ref[...] = basis
    kept_ref[...] = basis
    panel_cols = jnp.where(takes_ref[0] != 0, received_ref[...], held_ref[...])
    cols_ref[...] = dot(inverse, panel_cols, ((1,), (0,)))
    left = stack_left(basis)
    right = stack_right(2.0 * image_cols)
    chunk = 256
    for start in range(0, matrix_ref.shape[0], chunk):
        span = slice(start, start + chunk)
        begun_ref[span, :] = matrix_ref[span, :] - dot16(left[:, span], right, ((0,), (0,)))


def inner_kernel(ratio, which_ref, panel_ref, *refs):
    halves, (rows_ref, inner_ref) = refs[:ratio][::-1], refs[ratio:]
    width = inner_ref.shape[0]
    which = which_ref[0]
    parts = []
    for j in range(halves[0].shape[1] // width):
        span = slice(j * width, (j + 1) * width)
        for k in range(ratio):
            block = halves[0][:, span]
            for shift in range(1, ratio):
                block = jnp.where((which + shift) % ratio == k, halves[shift][:, span], block)
            parts.append(block)
    product_rows = jnp.concatenate(parts, axis=1)
    rows_ref[...] = product_rows
    inner_ref[...] = dot(panel_ref[...], product_rows, ((1,), (1,)))


def image_kernel(begun_ref, rows_ref, cols_ref, inverse_ref, further_ref, image_ref):
    image = dot(inverse_ref[...], rows_ref[...], ((1,), (0,)))
    image_ref[...] = image
    left = stack_left(2.0 * image)
    right = stack_right(cols_ref[...])
    chunk = 256
    for start in range(0, begun_ref.shape[0], chunk):
        span = slice(start, start + chunk)
        further_ref[span, :] = begun_ref[span, :] - dot16(left[:, span], right, ((0,), (0,)))


def update_kernel(
    further_ref, image_ref, basis_ref, cols_ref, inverse_ref, inner_ref, other_ref,
    updated_ref, w_ref, buffer_ref, w_buffer_ref, sems,
):
    inverse = inverse_ref[...]
    basis = basis_ref[...]
    inner = inner_ref[...] + other_ref[...]
    correction = dot(dot(inverse, inner, ((1,), (0,))), inverse, ((1,), (1,)))
    right = stack_right(4.0 * dot(correction, cols_ref[...], ((1,), (0,))))
    left = stack_left(basis)
    count = sems.shape[0] - 1
    chunk = further_ref.shape[0] // count
    copies = []
    for i in range(count):
        span = slice(i * chunk, (i + 1) * chunk)
        buffer_ref[span, :] = further_ref[span, :] + dot16(left[:, span], right, ((0,), (0,)))
        copies.append(
            pltpu.make_async_copy(buffer_ref.at[span, :], updated_ref.at[span, :], sems.at[i])
        )
        copies[-1].start()
    w_buffer_ref[...] = 2.0 * (image_ref[...] - dot(correction, basis, ((0,), (0,))))
    copies.append(pltpu.make_async_copy(w_buffer_ref, w_ref, sems.at[count]))
    copies[-1].start()
    for copy in copies:
        copy.wait()


def shape(*dims, dtype=jnp.float32):
    return jax.ShapeDtypeStruct(dims, dtype)


def call(kernel, outs, args, in_specs=None, out_specs=None, scratch=(), flops=0):
    return pl.pallas_call(
        kernel,
        out_shape=outs,
        in_specs=in_specs or [VMEM] * len(args),
        out_specs=out_specs or ((VMEM,) * len(outs) if isinstance(outs, tuple) else VMEM),
        scratch_shapes=scratch,
        compiler_params=PARAMS,
        cost_estimate=pl.CostEstimate(flops=flops, bytes_accessed=1 << 18, transcendentals=0),
    )(*args)


def local(matrix, panel):
    n_row, n_col = lax.axis_size("row"), lax.axis_size("col")
    ratio = n_col // n_row
    rows, width = panel.shape
    cols = matrix.shape[1]
    which = (lax.axis_index("col") // n_row).astype(jnp.int32).reshape(1)
    chunks = 8

    mine, panel_t, terms, gram, kept = call(
        functools.partial(panel_kernel, ratio),
        (
            shape(width, cols),
            shape(width, rows),
            shape(3 * width, rows, dtype=jnp.bfloat16),
            shape(STRIP, cols),
            shape(rows, cols),
        ),
        (
            which,
            pltpu.with_memory_space_constraint(panel.T, pltpu.HBM),
            pltpu.with_memory_space_constraint(matrix, pltpu.HBM),
        ),
        in_specs=[SMEM, HBM, HBM],
        scratch=[pltpu.SemaphoreType.DMA((2 * chunks,))],
        flops=1 << 28,
    )
    message = call(
        product_kernel, shape(width + STRIP, cols), (terms, kept, gram), flops=1 << 30
    )
    step = 1
    while 2 * step < n_row:
        message = message + partner(message, "row", step)
        step *= 2
    last = partner(message, "row", step)
    held, received, takes = spread_rows(mine, message)
    product_cols, gram = call(
        finish_kernel, (shape(width, cols), shape(width, width)), (last, message), flops=1 << 24
    )
    halves = [transpose_grid(product_cols, shift) for shift in reversed(range(ratio))]
    inverse = call(factor_kernel, shape(width, width), (gram,), flops=1 << 30)
    begun, basis, basis_kept, basis_cols = call(
        basis_kernel,
        (shape(rows, cols), shape(width, rows), shape(width, rows), shape(width, cols)),
        (kept, panel_t, product_cols, inverse, received, held, takes),
        in_specs=[VMEM] * 6 + [SMEM],
        flops=1 << 30,
    )
    halves, begun = lax.optimization_barrier((halves, begun))
    product_rows, inner = call(
        functools.partial(inner_kernel, ratio),
        (shape(width, rows), shape(width, width)),
        (which, panel_t, *halves),
        in_specs=[SMEM] + [VMEM] * (1 + ratio),
        flops=1 << 24,
    )
    further, image = call(
        image_kernel,
        (shape(rows, cols), shape(width, rows)),
        (begun, product_rows, basis_cols, inverse),
        flops=1 << 30,
    )
    step = 1
    while 2 * step < n_row:
        inner = inner + partner(inner, "row", step)
        step *= 2
    updated, w_rows = call(
        update_kernel,
        (shape(rows, cols), shape(width, rows)),
        (further, image, basis_kept, basis_cols, inverse, inner, partner(inner, "row", step)),
        out_specs=(HBM, HBM),
        scratch=[
            pltpu.VMEM((rows, cols), jnp.float32),
            pltpu.VMEM((width, rows), jnp.float32),
            pltpu.SemaphoreType.DMA((chunks + 1,)),
        ],
        flops=1 << 30,
    )
    return (updated, w_rows.T, basis.T)


def solution(mesh):
    return jax.shard_map(
        local,
        mesh=mesh,
        in_specs=(P("row", "col"), P("row", None)),
        out_specs=(P("row", "col"), P("row", None), P("row", None)),
        check_vma=False,
    )
```

profile of v0, /device:TPU:0, one launch (start us, length us, event | category | flops | bytes accessed | tf_op | source)
XLA Modules:
  0.0 30.5 jit_solution(12670473210513254286)
XLA Ops:
  0.6 1.8 %shard_map.49 = (f32[64,512]{1,0:T(8,128)S(1)}, f32[64,1024]{1,0:T(8,128)S(1)}, bf16[192,1024]{1,0:T(8,128)(2,1)S(1)}, f32[8,512]{1,0:T(8,128)S(1)}, f32[1024,512]{1,0:T(8,128)S(1)}) custom-call(s32[1]{0:T(128)} %bitcast.which_ref, f32[64,1024]{1,0:T(8,128)} %bitcast.5, f32[1024,512]{1,0:T(8,128)} %matrix_ref.1), custom_call_target="tpu_custom_call" | custom-call | flops 268435456 | bytes 262144 | tf_op jit(solution)/shard_map/pallas_call | solution.py:265
  2.5 0.8 %shard_map.50 = f32[72,512]{1,0:T(8,128)S(1)} custom-call(bf16[192,1024]{1,0:T(8,128)(2,1)S(1)} %get-tuple-element.24.terms_ref, f32[1024,512]{1,0:T(8,128)S(1)} %get-tuple-element.25.matrix_ref, f32[8,512]{1,0:T(8,128)S(1)} %get-tuple-element.26.gram_ref), custom_call_target="tpu_custom_call" | custom-call | flops 1073741824 | bytes 262144 | tf_op jit(solution)/shard_map/pallas_call | solution.py:265
  3.3 0.5 %collective-permute-start = (f32[72,512]{1,0:T(8,128)S(1)}, f32[72,512]{1,0:T(8,128)S(1)}, u32[]{:S(2)}, u32[]{:S(2)}) collective-permute-start(f32[72,512]{1,0:T(8,128)S(1)} %shard_map.50), channel_id=1, source_target_pairs={{0,8},{8,0},{16,24},{24,16},{1,9},{9,1},{17,25},{25,17},{2,10},{10... | collective-permute-start | bytes 442376 | tf_op jit(solution)/shard_map/ppermute | solution.py:38
  3.8 2.0 %collective-permute-start.4 = (f32[64,512]{1,0:T(8,128)S(1)}, f32[64,512]{1,0:T(8,128)S(1)}, u32[]{:S(2)}, u32[]{:S(2)}) collective-permute-start(f32[64,512]{1,0:T(8,128)S(1)} %get-tuple-element.30), channel_id=1, source_target_pairs={{0,8},{9,1},{18,26},{27,19},{4,12},{13,5},{22,30},{31,23}} | collective-permute-start | bytes 393224 | tf_op jit(solution)/shard_map/ppermute | solution.py:53
  5.8 0.0 collective-permute-done
  5.8 2.0 %collective-permute-start.1 = (f32[72,512]{1,0:T(8,128)S(1)}, f32[72,512]{1,0:T(8,128)S(1)}, u32[]{:S(2)}, u32[]{:S(2)}) collective-permute-start(f32[72,512]{1,0:T(8,128)S(1)} %add.11.mine_ref), channel_id=1, source_target_pairs={{0,16},{8,24},{16,0},{24,8},{1,17},{9,25},{17,1},{25,9},{2,18},{10... | collective-permute-start | bytes 442376 | tf_op jit(solution)/shard_map/ppermute | solution.py:38
  7.8 0.0 collective-permute-done.4
  7.8 2.0 %collective-permute-start.5 = (f32[64,512]{1,0:T(8,128)S(1)}, f32[64,512]{1,0:T(8,128)S(1)}, u32[]{:S(2)}, u32[]{:S(2)}) collective-permute-start(f32[64,512]{1,0:T(8,128)S(1)} %broadcast_select_fusion.held_ref), channel_id=1, source_target_pairs={{0,16},{8,24},{9,25},{1,17},{18,2},{26,10},{27,11},{19,3},{4,20},{... | collective-permute-start | bytes 393224 | tf_op jit(solution)/shard_map/ppermute | solution.py:53
  9.8 2.1 %collective-permute-done.1.other_ref = f32[72,512]{1,0:T(8,128)S(1)} collective-permute-done((f32[72,512]{1,0:T(8,128)S(1)}, f32[72,512]{1,0:T(8,128)S(1)}, u32[]{:S(2)}, u32[]{:S(2)}) %collective-permute-start.1) | collective-permute-done | bytes 147488 | tf_op jit(solution)/shard_map/ppermute | solution.py:38
  12.0 0.1 shard_map.51
  12.1 3.1 %collective-permute-start.2 = (f32[64,512]{1,0:T(8,128)S(1)}, f32[64,512]{1,0:T(8,128)S(1)}, u32[]{:S(2)}, u32[]{:S(2)}) collective-permute-start(f32[64,512]{1,0:T(8,128)S(1)} %get-tuple-element.27.product_cols_ref), channel_id=1, source_target_pairs={{4,0},{12,1},{20,2},{28,3},{0,4},{8,5},{16,6},{24,7},{5,8},{13,9},... | collective-permute-start | bytes 393224 | tf_op jit(solution)/shard_map/ppermute | solution.py:71
  15.1 1.8 %collective-permute-start.3 = (f32[64,512]{1,0:T(8,128)S(1)}, f32[64,512]{1,0:T(8,128)S(1)}, u32[]{:S(2)}, u32[]{:S(2)}) collective-permute-start(f32[64,512]{1,0:T(8,128)S(1)} %get-tuple-element.27.product_cols_ref), channel_id=1, source_target_pairs={{16,0},{24,1},{0,2},{8,3},{20,4},{28,5},{4,6},{12,7},{17,8},{25,9}... | collective-permute-start | bytes 393224 | tf_op jit(solution)/shard_map/ppermute | solution.py:71
  17.0 2.8 %shard_map.52.inverse_ref = f32[64,64]{1,0:T(8,128)S(1)} custom-call(f32[64,64]{1,0:T(8,128)S(1)} %get-tuple-element.29.gram_ref), custom_call_target="tpu_custom_call" | custom-call | flops 1073741824 | bytes 262144 | tf_op jit(solution)/shard_map/pallas_call | solution.py:265
  19.8 0.0 collective-permute-done.5.received_ref
  19.8 1.1 %shard_map.53 = (f32[1024,512]{1,0:T(8,128)S(1)}, f32[64,1024]{1,0:T(8,128)}, f32[64,1024]{1,0:T(8,128)S(1)}, f32[64,512]{1,0:T(8,128)S(1)}) custom-call(f32[1024,512]{1,0:T(8,128)S(1)} %get-tuple-element.25.matrix_ref, f32[64,1024]{1,0:T(8,128)S(1)} %get-tuple-element.28.panel_ref, f32[64,512]{1,0:T(8,128)S(1)} %get-tuple-element.27.product_cols_ref, ...), custom_call_target="tpu_custom_call" | custom-call | flops 1073741824 | bytes 262144 | tf_op jit(solution)/shard_map/pallas_call | solution.py:265
  20.9 0.0 collective-permute-done.2.refs_0_
  20.9 0.3 %collective-permute-done.3.refs_1_ = f32[64,512]{1,0:T(8,128)S(1)} collective-permute-done((f32[64,512]{1,0:T(8,128)S(1)}, f32[64,512]{1,0:T(8,128)S(1)}, u32[]{:S(2)}, u32[]{:S(2)}) %collective-permute-start.3) | collective-permute-done | bytes 131104 | tf_op jit(solution)/shard_map/ppermute | solution.py:71
  21.2 0.4 %shard_map.54 = (f32[64,1024]{1,0:T(8,128)S(1)}, f32[64,64]{1,0:T(8,128)S(1)}) custom-call(s32[1]{0:T(128)} %bitcast.which_ref, f32[64,1024]{1,0:T(8,128)S(1)} %get-tuple-element.28.panel_ref, f32[64,512]{1,0:T(8,128)S(1)} %collective-permute-done.2.refs_0_, f32[64,512]{1,0:T(8,128)S(1)} %collective-permute-done.3.refs_1_), custom_call_target="tpu_custom_call" | custom-call | flops 16777216 | bytes 262144 | tf_op jit(solution)/shard_map/pallas_call | solution.py:265
  21.7 1.8 %collective-permute-start.6 = (f32[64,64]{1,0:T(8,128)S(1)}, f32[64,64]{1,0:T(8,128)S(1)}, u32[]{:S(2)}, u32[]{:S(2)}) collective-permute-start(f32[64,64]{1,0:T(8,128)S(1)} %get-tuple-element.41), channel_id=1, source_target_pairs={{0,8},{8,0},{16,24},{24,16},{1,9},{9,1},{17,25},{25,17},{2,10},{10... | collective-permute-start | bytes 49160 | tf_op jit(solution)/shard_map/ppermute | solution.py:38
  23.4 0.9 %collective-permute-done.6 = f32[64,64]{1,0:T(8,128)S(1)} collective-permute-done((f32[64,64]{1,0:T(8,128)S(1)}, f32[64,64]{1,0:T(8,128)S(1)}, u32[]{:S(2)}, u32[]{:S(2)}) %collective-permute-start.6) | collective-permute-done | bytes 16416 | tf_op jit(solution)/shard_map/ppermute | solution.py:38
  24.3 1.5 %collective-permute-start.7 = (f32[64,64]{1,0:T(8,128)S(1)}, f32[64,64]{1,0:T(8,128)S(1)}, u32[]{:S(2)}, u32[]{:S(2)}) collective-permute-start(f32[64,64]{1,0:T(8,128)S(1)} %add.13.inner_ref), channel_id=1, source_target_pairs={{0,16},{8,24},{16,0},{24,8},{1,17},{9,25},{17,1},{25,9},{2,18},{10... | collective-permute-start | bytes 49160 | tf_op jit(solution)/shard_map/ppermute | solution.py:38
  25.7 0.7 %shard_map.55 = (f32[1024,512]{1,0:T(8,128)S(1)}, f32[64,1024]{1,0:T(8,128)S(1)}) custom-call(f32[1024,512]{1,0:T(8,128)S(1)} %get-tuple-element.33.begun_ref, f32[64,1024]{1,0:T(8,128)S(1)} %get-tuple-element.36.rows_ref, f32[64,512]{1,0:T(8,128)S(1)} %get-tuple-element.37.cols_ref, f32[64,64]{1,0:T(8,128)S(1)} %shard_map.52.inverse_ref), custom_call_target="tpu_custom_call" | custom-call | flops 1073741824 | bytes 262144 | tf_op jit(solution)/shard_map/pallas_call | solution.py:265
  26.5 1.7 %collective-permute-done.7.other_ref = f32[64,64]{1,0:T(8,128)S(1)} collective-permute-done((f32[64,64]{1,0:T(8,128)S(1)}, f32[64,64]{1,0:T(8,128)S(1)}, u32[]{:S(2)}, u32[]{:S(2)}) %collective-permute-start.7) | collective-permute-done | bytes 16416 | tf_op jit(solution)/shard_map/ppermute | solution.py:38
  28.2 2.3 %shard_map.56 = (f32[1024,512]{1,0:T(8,128)}, f32[64,1024]{1,0:T(8,128)}) custom-call(f32[1024,512]{1,0:T(8,128)S(1)} %get-tuple-element.38.further_ref, f32[64,1024]{1,0:T(8,128)S(1)} %get-tuple-element.39.image_ref, f32[64,1024]{1,0:T(8,128)S(1)} %get-tuple-element.40.basis_ref, f32[64,512]{1,0:T(8,128)S(1)} %get-tuple-element.37.cols_ref, ...), custom_call_target="tpu_custom_call" | custom-call | flops 1073741824 | bytes 262144 | tf_op jit(solution)/shard_map/pallas_call | solution.py:265
  (3 shorter events, 0.0 us)
Async XLA Ops:
  3.3 2.5 %collective-permute-start = (f32[72,512]{1,0:T(8,128)S(1)}, f32[72,512]{1,0:T(8,128)S(1)}, u32[]{:S(2)}, u32[]{:S(2)}) collective-permute-start(f32[72,512]{1,0:T(8,128)S(1)} %shard_map.50), channel_id=1, source_target_pairs={{0,8},{8,0},{16,24},{24,16},{1,9},{9,1},{17,25},{25,17},{2,10},{10... | collective-permute-start | bytes 442376 | tf_op jit(solution)/shard_map/ppermute | solution.py:38
  3.8 4.0 %collective-permute-start.4 = (f32[64,512]{1,0:T(8,128)S(1)}, f32[64,512]{1,0:T(8,128)S(1)}, u32[]{:S(2)}, u32[]{:S(2)}) collective-permute-start(f32[64,512]{1,0:T(8,128)S(1)} %get-tuple-element.30), channel_id=1, source_target_pairs={{0,8},{9,1},{18,26},{27,19},{4,12},{13,5},{22,30},{31,23}} | collective-permute-start | bytes 393224 | tf_op jit(solution)/shard_map/ppermute | solution.py:53
  5.8 6.2 %collective-permute-start.1 = (f32[72,512]{1,0:T(8,128)S(1)}, f32[72,512]{1,0:T(8,128)S(1)}, u32[]{:S(2)}, u32[]{:S(2)}) collective-permute-start(f32[72,512]{1,0:T(8,128)S(1)} %add.11.mine_ref), channel_id=1, source_target_pairs={{0,16},{8,24},{16,0},{24,8},{1,17},{9,25},{17,1},{25,9},{2,18},{10... | collective-permute-start | bytes 442376 | tf_op jit(solution)/shard_map/ppermute | solution.py:38
  7.8 12.0 %collective-permute-start.5 = (f32[64,512]{1,0:T(8,128)S(1)}, f32[64,512]{1,0:T(8,128)S(1)}, u32[]{:S(2)}, u32[]{:S(2)}) collective-permute-start(f32[64,512]{1,0:T(8,128)S(1)} %broadcast_select_fusion.held_ref), channel_id=1, source_target_pairs={{0,16},{8,24},{9,25},{1,17},{18,2},{26,10},{27,11},{19,3},{4,20},{... | collective-permute-start | bytes 393224 | tf_op jit(solution)/shard_map/ppermute | solution.py:53
  12.1 8.8 %collective-permute-start.2 = (f32[64,512]{1,0:T(8,128)S(1)}, f32[64,512]{1,0:T(8,128)S(1)}, u32[]{:S(2)}, u32[]{:S(2)}) collective-permute-start(f32[64,512]{1,0:T(8,128)S(1)} %get-tuple-element.27.product_cols_ref), channel_id=1, source_target_pairs={{4,0},{12,1},{20,2},{28,3},{0,4},{8,5},{16,6},{24,7},{5,8},{13,9},... | collective-permute-start | bytes 393224 | tf_op jit(solution)/shard_map/ppermute | solution.py:71
  15.1 6.1 %collective-permute-start.3 = (f32[64,512]{1,0:T(8,128)S(1)}, f32[64,512]{1,0:T(8,128)S(1)}, u32[]{:S(2)}, u32[]{:S(2)}) collective-permute-start(f32[64,512]{1,0:T(8,128)S(1)} %get-tuple-element.27.product_cols_ref), channel_id=1, source_target_pairs={{16,0},{24,1},{0,2},{8,3},{20,4},{28,5},{4,6},{12,7},{17,8},{25,9}... | collective-permute-start | bytes 393224 | tf_op jit(solution)/shard_map/ppermute | solution.py:71
  21.7 2.6 %collective-permute-start.6 = (f32[64,64]{1,0:T(8,128)S(1)}, f32[64,64]{1,0:T(8,128)S(1)}, u32[]{:S(2)}, u32[]{:S(2)}) collective-permute-start(f32[64,64]{1,0:T(8,128)S(1)} %get-tuple-element.41), channel_id=1, source_target_pairs={{0,8},{8,0},{16,24},{24,16},{1,9},{9,1},{17,25},{25,17},{2,10},{10... | collective-permute-start | bytes 49160 | tf_op jit(solution)/shard_map/ppermute | solution.py:38
  24.3 3.9 %collective-permute-start.7 = (f32[64,64]{1,0:T(8,128)S(1)}, f32[64,64]{1,0:T(8,128)S(1)}, u32[]{:S(2)}, u32[]{:S(2)}) collective-permute-start(f32[64,64]{1,0:T(8,128)S(1)} %add.13.inner_ref), channel_id=1, source_target_pairs={{0,16},{8,24},{16,0},{24,8},{1,17},{9,25},{17,1},{25,9},{2,18},{10... | collective-permute-start | bytes 49160 | tf_op jit(solution)/shard_map/ppermute | solution.py:38
where the time goes:
time: 30.7 us; the launch traced here: 30.5 us
  starting transfers between devices  14.6 us (48%)
  Pallas kernels  10.1 us (33%)
  waiting for transfers between devices  5.02 us (16%)
  between operations  0.75 us (2%)
    pallas_call x8, Pallas kernels, call(): pl.pallas_call(kernel, out_shape=outs, in_specs=in_specs or [VMEM] * len(...  10.1 us
    ppermute x4, starting transfers between devices, partner(): return lax.ppermute(value, axis, [(i, i ^ step) for i in range(size)])  5.69 us
    ppermute x2, starting transfers between devices, transpose_grid(): return lax.ppermute(value, ('row', 'col'), pairs)  4.91 us
    ppermute x4, waiting for transfers between devices, partner(): return lax.ppermute(value, axis, [(i, i ^ step) for i in range(size)])  4.7 us
    ppermute x2, starting transfers between devices, spread_rows(): received = lax.ppermute(value, ('row', 'col'), pairs)  4.01 us
  transfers between devices with their start and end apart: 8, of which 4 were waited for; matrix products, arithmetic and copies ran while one was open for 0% of the time, Pallas kernels for 16%

commit v1 on v0

--- a/solution.py
+++ b/solution.py
@@ -83,10 +83,8 @@
     return copies
 
 
-def panel_kernel(
-    ratio, which_ref, panel_ref, matrix_ref,
-    mine_ref, held_ref, terms_ref, gram_ref, kept_ref, sems,
-):
+def panel_kernel(ratio, which_ref, panel_ref, matrix_ref, *refs):
+    mine_refs, (held_ref, terms_ref, gram_ref, kept_ref, sems) = refs[:ratio], refs[ratio:]
     width = panel_ref.shape[0]
     pieces = sems.shape[0] // 2
     panel_copies = copy_rows(panel_ref, held_ref, sems, 0, pieces)
@@ -94,13 +92,14 @@
     for copy in panel_copies:
         copy.wait()
     which = which_ref[0]
-    for j in range(mine_ref.shape[1] // width):
+    for j in range(mine_refs[0].shape[1] // width):
         start = j * ratio * width
-        block = held_ref[:, start : start + width]
-        for k in range(1, ratio):
-            start += width
-            block = jnp.where(which == k, held_ref[:, start : start + width], block)
-        mine_ref[:, j * width : (j + 1) * width] = block
+        blocks = [held_ref[:, start + k * width : start + (k + 1) * width] for k in range(ratio)]
+        for shift, mine_ref in enumerate(mine_refs):
+            block = blocks[shift]
+            for k in range(1, ratio):
+                block = jnp.where(which == k, blocks[(k + shift) % ratio], block)
+            mine_ref[:, j * width : (j + 1) * width] = block
     panel = held_ref[...]
     terms_ref[...] = jnp.concatenate(split(panel, 3), axis=0)
     to_strip(dot(panel, panel, ((1,), (1,))), gram_ref)
@@ -185,16 +184,19 @@
 
 def basis_kernel(
     matrix_ref, panel_ref, product_cols_ref, inverse_ref, received_ref, held_ref, takes_ref,
-    begun_ref, basis_ref, kept_ref, cols_ref,
+    begun_ref, basis_ref, left_ref, coeffs_ref, cols_ref, coeffs_cols_ref,
 ):
     inverse = inverse_ref[...]
     basis = dot(inverse, panel_ref[...], ((1,), (0,)))
     image_cols = dot(inverse, product_cols_ref[...], ((1,), (0,)))
     basis_ref[...] = basis
-    kept_ref[...] = basis
+    coeffs_ref[...] = dot(inverse, basis, ((0,), (0,)))
     panel_cols = jnp.where(takes_ref[0] != 0, received_ref[...], held_ref[...])
-    cols_ref[...] = dot(inverse, panel_cols, ((1,), (0,)))
+    cols = dot(inverse, panel_cols, ((1,), (0,)))
+    cols_ref[...] = cols
+    coeffs_cols_ref[...] = dot(inverse, cols, ((0,), (0,)))
     left = stack_left(basis)
+    left_ref[...] = left
     right = stack_right(2.0 * image_cols)
     chunk = 256
     for start in range(0, matrix_ref.shape[0], chunk):
@@ -202,9 +204,17 @@
         begun_ref[span, :] = matrix_ref[span, :] - dot16(left[:, span], right, ((0,), (0,)))
 
 
-def inner_kernel(ratio, which_ref, panel_ref, *refs):
-    halves, (rows_ref, inner_ref) = refs[:ratio][::-1], refs[ratio:]
-    width = inner_ref.shape[0]
+def inner_kernel(*refs):
+    count = len(refs) // 2
+    inner_ref = refs[-1]
+    inner_ref[...] = sum(
+        dot(refs[count + i][...], refs[i][...], ((1,), (1,))) for i in range(count)
+    )
+
+
+def image_kernel(ratio, which_ref, begun_ref, cols_ref, inverse_ref, *refs):
+    halves, (further_ref, image_ref) = refs[:ratio][::-1], refs[ratio:]
+    width = inverse_ref.shape[0]
     which = which_ref[0]
     parts = []
     for j in range(halves[0].shape[1] // width):
@@ -214,13 +224,7 @@
             for shift in range(1, ratio):
                 block = jnp.where((which + shift) % ratio == k, halves[shift][:, span], block)
             parts.append(block)
-    product_rows = jnp.concatenate(parts, axis=1)
-    rows_ref[...] = product_rows
-    inner_ref[...] = dot(panel_ref[...], product_rows, ((1,), (1,)))
-
-
-def image_kernel(begun_ref, rows_ref, cols_ref, inverse_ref, further_ref, image_ref):
-    image = dot(inverse_ref[...], rows_ref[...], ((1,), (0,)))
+    image = dot(inverse_ref[...], jnp.concatenate(parts, axis=1), ((1,), (0,)))
     image_ref[...] = image
     left = stack_left(2.0 * image)
     right = stack_right(cols_ref[...])
@@ -231,26 +235,25 @@
 
 
 def update_kernel(
-    further_ref, image_ref, basis_ref, cols_ref, inverse_ref, inner_ref, other_ref,
-    updated_ref, w_ref, buffer_ref, w_buffer_ref, sems,
+    further_ref, image_ref, left_ref, coeffs_ref, coeffs_cols_ref, inverse_ref,
+    inner_ref, other_ref, updated_ref, w_ref, buffer_ref, w_buffer_ref, sems,
 ):
     inverse = inverse_ref[...]
-    basis = basis_ref[...]
     inner = inner_ref[...] + other_ref[...]
-    correction = dot(dot(inverse, inner, ((1,), (0,))), inverse, ((1,), (1,)))
-    right = stack_right(4.0 * dot(correction, cols_ref[...], ((1,), (0,))))
-    left = stack_left(basis)
+    right = dot(inverse, dot(inner, coeffs_cols_ref[...], ((1,), (0,))), ((1,), (0,)))
+    right = stack_right(4.0 * right)
     count = sems.shape[0] - 1
     chunk = further_ref.shape[0] // count
     copies = []
     for i in range(count):
         span = slice(i * chunk, (i + 1) * chunk)
-        buffer_ref[span, :] = further_ref[span, :] + dot16(left[:, span], right, ((0,), (0,)))
+        buffer_ref[span, :] = further_ref[span, :] + dot16(left_ref[:, span], right, ((0,), (0,)))
         copies.append(
             pltpu.make_async_copy(buffer_ref.at[span, :], updated_ref.at[span, :], sems.at[i])
         )
         copies[-1].start()
-    w_buffer_ref[...] = 2.0 * (image_ref[...] - dot(correction, basis, ((0,), (0,))))
+    removed = dot(inverse, dot(inner, coeffs_ref[...], ((0,), (0,))), ((1,), (0,)))
+    w_buffer_ref[...] = 2.0 * (image_ref[...] - removed)
     copies.append(pltpu.make_async_copy(w_buffer_ref, w_ref, sems.at[count]))
     copies[-1].start()
     for copy in copies:
@@ -281,10 +284,10 @@
     which = (lax.axis_index("col") // n_row).astype(jnp.int32).reshape(1)
     chunks = 8
 
-    mine, panel_t, terms, gram, kept = call(
+    *mines, panel_t, terms, gram, kept = call(
         functools.partial(panel_kernel, ratio),
         (
-            shape(width, cols),
+            *[shape(width, cols)] * ratio,
             shape(width, rows),
             shape(3 * width, rows, dtype=jnp.bfloat16),
             shape(STRIP, cols),
@@ -307,31 +310,33 @@
         message = message + partner(message, "row", step)
         step *= 2
     last = partner(message, "row", step)
-    held, received, takes = spread_rows(mine, message)
+    held, received, takes = spread_rows(mines[0], message)
     product_cols, gram = call(
         finish_kernel, (shape(width, cols), shape(width, width)), (last, message), flops=1 << 24
     )
     halves = [transpose_grid(product_cols, shift) for shift in reversed(range(ratio))]
     inverse = call(factor_kernel, shape(width, width), (gram,), flops=1 << 30)
-    begun, basis, basis_kept, basis_cols = call(
+    begun, basis, left, coeffs, basis_cols, coeffs_cols = call(
         basis_kernel,
-        (shape(rows, cols), shape(width, rows), shape(width, rows), shape(width, cols)),
+        (
+            shape(rows, cols),
+            shape(width, rows),
+            shape(3 * width, rows, dtype=jnp.bfloat16),
+            shape(width, rows),
+            shape(width, cols),
+            shape(width, cols),
+        ),
         (kept, panel_t, product_cols, inverse, received, held, takes),
         in_specs=[VMEM] * 6 + [SMEM],
         flops=1 << 30,
     )
     halves, begun = lax.optimization_barrier((halves, begun))
-    product_rows, inner = call(
-        functools.partial(inner_kernel, ratio),
-        (shape(width, rows), shape(width, width)),
-        (which, panel_t, *halves),
-        in_specs=[SMEM] + [VMEM] * (1 + ratio),
-        flops=1 << 24,
-    )
+    inner = call(inner_kernel, shape(width, width), (*halves, *mines[::-1]), flops=1 << 24)
     further, image = call(
-        image_kernel,
+        functools.partial(image_kernel, ratio),
         (shape(rows, cols), shape(width, rows)),
-        (begun, product_rows, basis_cols, inverse),
+        (which, begun, basis_cols, inverse, *halves),
+        in_specs=[SMEM] + [VMEM] * (3 + ratio),
         flops=1 << 30,
     )
     step = 1
@@ -341,7 +346,10 @@
     updated, w_rows = call(
         update_kernel,
         (shape(rows, cols), shape(width, rows)),
-        (further, image, basis_kept, basis_cols, inverse, inner, partner(inner, "row", step)),
+        (
+            further, image, left, coeffs, coeffs_cols, inverse,
+            inner, partner(inner, "row", step),
+        ),
         out_specs=(HBM, HBM),
         scratch=[
             pltpu.VMEM((rows, cols), jnp.float32),

time: 30.7 us -> 30.5 us (level)
  waiting for transfers between devices: 5.02 us -> 4.65 us
    ppermute x2, waiting for transfers between devices: 0.31 us -> 0.01 us  [transpose_grid(): return lax.ppermute(value, ('row', 'col'), pairs)]
  transfers between devices with their start and end apart: 8 -> 8, of which waited for: 4 -> 3; matrix products, arithmetic and copies ran while one was open for 0% -> 0% of each run, Pallas kernels for 16% -> 17%
where the time goes in v1:
time: 30.5 us; the launch traced here: 30.3 us
  starting transfers between devices  14.6 us (48%)
  Pallas kernels  10.2 us (33%)
  waiting for transfers between devices  4.65 us (15%)
  between operations  0.77 us (3%)
    pallas_call x8, Pallas kernels, call(): pl.pallas_call(kernel, out_shape=outs, in_specs=in_specs or [VMEM] * len(...  10.2 us
    ppermute x4, starting transfers between devices, partner(): return lax.ppermute(value, axis, [(i, i ^ step) for i in range(size)])  5.68 us
    ppermute x2, starting transfers between devices, transpose_grid(): return lax.ppermute(value, ('row', 'col'), pairs)  4.91 us
    ppermute x4, waiting for transfers between devices, partner(): return lax.ppermute(value, axis, [(i, i ^ step) for i in range(size)])  4.63 us
    ppermute x2, starting transfers between devices, spread_rows(): received = lax.ppermute(value, ('row', 'col'), pairs)  4.01 us
  transfers between devices with their start and end apart: 8, of which 3 were waited for; matrix products, arithmetic and copies ran while one was open for 0% of the time, Pallas kernels for 17%

profile of v1, /device:TPU:0, one launch (start us, length us, event | category | flops | bytes accessed | tf_op | source)
XLA Modules:
  0.0 30.3 jit_solution(12327602758143137678)
XLA Ops:
  0.6 1.8 %shard_map.49 = (f32[64,512]{1,0:T(8,128)S(1)}, f32[64,512]{1,0:T(8,128)S(1)}, f32[64,1024]{1,0:T(8,128)S(1)}, bf16[192,1024]{1,0:T(8,128)(2,1)S(1)}, f32[8,512]{1,0:T(8,128)S(1)}, /*index=5*/f32[1024,512]{1,0:T(8,128)S(1)}) custom-call(s32[1]{0:T(128)} %bitcast.which_ref, f32[64,1024]{1,0:T(8,128)} %bitcast.5, f32[1024,512]{1,0:T(8,128)} %matrix_ref.1), custom_call_target="tpu_custom_call" | custom-call | flops 268435456 | bytes 262144 | tf_op jit(solution)/shard_map/pallas_call | solution.py:268
  2.5 0.8 %shard_map.50 = f32[72,512]{1,0:T(8,128)S(1)} custom-call(bf16[192,1024]{1,0:T(8,128)(2,1)S(1)} %get-tuple-element.25.terms_ref, f32[1024,512]{1,0:T(8,128)S(1)} %get-tuple-element.26.matrix_ref, f32[8,512]{1,0:T(8,128)S(1)} %get-tuple-element.27.gram_ref), custom_call_target="tpu_custom_call" | custom-call | flops 1073741824 | bytes 262144 | tf_op jit(solution)/shard_map/pallas_call | solution.py:268
  3.3 0.5 %collective-permute-start = (f32[72,512]{1,0:T(8,128)S(1)}, f32[72,512]{1,0:T(8,128)S(1)}, u32[]{:S(2)}, u32[]{:S(2)}) collective-permute-start(f32[72,512]{1,0:T(8,128)S(1)} %shard_map.50), channel_id=1, source_target_pairs={{0,8},{8,0},{16,24},{24,16},{1,9},{9,1},{17,25},{25,17},{2,10},{10... | collective-permute-start | bytes 442376 | tf_op jit(solution)/shard_map/ppermute | solution.py:38
  3.8 2.0 %collective-permute-start.4 = (f32[64,512]{1,0:T(8,128)S(1)}, f32[64,512]{1,0:T(8,128)S(1)}, u32[]{:S(2)}, u32[]{:S(2)}) collective-permute-start(f32[64,512]{1,0:T(8,128)S(1)} %get-tuple-element.31.refs_3_), channel_id=1, source_target_pairs={{0,8},{9,1},{18,26},{27,19},{4,12},{13,5},{22,30},{31,23}} | collective-permute-start | bytes 393224 | tf_op jit(solution)/shard_map/ppermute | solution.py:53
  5.8 0.0 collective-permute-done
  5.8 2.0 %collective-permute-start.1 = (f32[72,512]{1,0:T(8,128)S(1)}, f32[72,512]{1,0:T(8,128)S(1)}, u32[]{:S(2)}, u32[]{:S(2)}) collective-permute-start(f32[72,512]{1,0:T(8,128)S(1)} %add.11.mine_ref), channel_id=1, source_target_pairs={{0,16},{8,24},{16,0},{24,8},{1,17},{9,25},{17,1},{25,9},{2,18},{10... | collective-permute-start | bytes 442376 | tf_op jit(solution)/shard_map/ppermute | solution.py:38
  7.8 0.0 collective-permute-done.4
  7.8 2.0 %collective-permute-start.5 = (f32[64,512]{1,0:T(8,128)S(1)}, f32[64,512]{1,0:T(8,128)S(1)}, u32[]{:S(2)}, u32[]{:S(2)}) collective-permute-start(f32[64,512]{1,0:T(8,128)S(1)} %broadcast_select_fusion.held_ref), channel_id=1, source_target_pairs={{0,16},{8,24},{9,25},{1,17},{18,2},{26,10},{27,11},{19,3},{4,20},{... | collective-permute-start | bytes 393224 | tf_op jit(solution)/shard_map/ppermute | solution.py:53
  9.8 2.1 %collective-permute-done.1.other_ref = f32[72,512]{1,0:T(8,128)S(1)} collective-permute-done((f32[72,512]{1,0:T(8,128)S(1)}, f32[72,512]{1,0:T(8,128)S(1)}, u32[]{:S(2)}, u32[]{:S(2)}) %collective-permute-start.1) | collective-permute-done | bytes 147488 | tf_op jit(solution)/shard_map/ppermute | solution.py:38
  12.0 0.1 shard_map.51
  12.1 3.1 %collective-permute-start.2 = (f32[64,512]{1,0:T(8,128)S(1)}, f32[64,512]{1,0:T(8,128)S(1)}, u32[]{:S(2)}, u32[]{:S(2)}) collective-permute-start(f32[64,512]{1,0:T(8,128)S(1)} %get-tuple-element.28.product_cols_ref), channel_id=1, source_target_pairs={{4,0},{12,1},{20,2},{28,3},{0,4},{8,5},{16,6},{24,7},{5,8},{13,9},... | collective-permute-start | bytes 393224 | tf_op jit(solution)/shard_map/ppermute | solution.py:71
  15.1 1.8 %collective-permute-start.3 = (f32[64,512]{1,0:T(8,128)S(1)}, f32[64,512]{1,0:T(8,128)S(1)}, u32[]{:S(2)}, u32[]{:S(2)}) collective-permute-start(f32[64,512]{1,0:T(8,128)S(1)} %get-tuple-element.28.product_cols_ref), channel_id=1, source_target_pairs={{16,0},{24,1},{0,2},{8,3},{20,4},{28,5},{4,6},{12,7},{17,8},{25,9}... | collective-permute-start | bytes 393224 | tf_op jit(solution)/shard_map/ppermute | solution.py:71
  17.0 2.8 %shard_map.52.inverse_ref = f32[64,64]{1,0:T(8,128)S(1)} custom-call(f32[64,64]{1,0:T(8,128)S(1)} %get-tuple-element.30.gram_ref), custom_call_target="tpu_custom_call" | custom-call | flops 1073741824 | bytes 262144 | tf_op jit(solution)/shard_map/pallas_call | solution.py:268
  19.8 0.0 collective-permute-done.5.received_ref
  19.8 1.4 %shard_map.53 = (f32[1024,512]{1,0:T(8,128)S(1)}, f32[64,1024]{1,0:T(8,128)}, bf16[192,1024]{1,0:T(8,128)(2,1)S(1)}, f32[64,1024]{1,0:T(8,128)S(1)}, f32[64,512]{1,0:T(8,128)S(1)}, /*index=5*/f32[64,512]{1,0:T(8,128)S(1)}) custom-call(f32[1024,512]{1,0:T(8,128)S(1)} %get-tuple-element.26.matrix_ref, f32[64,1024]{1,0:T(8,128)S(1)} %get-tuple-element.29.panel_ref, ...), custom_call_target="tpu_custom_call" | custom-call | flops 1073741824 | bytes 262144 | tf_op jit(solution)/shard_map/pallas_call | solution.py:268
  21.2 0.0 collective-permute-done.2.refs_0_
  21.2 0.0 collective-permute-done.3.refs_1_
  21.2 0.4 %shard_map.55 = f32[64,64]{1,0:T(8,128)S(1)} custom-call(f32[64,512]{1,0:T(8,128)S(1)} %collective-permute-done.2.refs_0_, f32[64,512]{1,0:T(8,128)S(1)} %collective-permute-done.3.refs_1_, f32[64,512]{1,0:T(8,128)S(1)} %get-tuple-element.43.refs_2_, f32[64,512]{1,0:T(8,128)S(1)} %get-tuple-element.31.refs_3_), custom_call_target="tpu_custom_call" | custom-call | flops 16777216 | bytes 262144 | tf_op jit(solution)/shard_map/pallas_call | solution.py:268
  21.6 1.7 %collective-permute-start.6 = (f32[64,64]{1,0:T(8,128)S(1)}, f32[64,64]{1,0:T(8,128)S(1)}, u32[]{:S(2)}, u32[]{:S(2)}) collective-permute-start(f32[64,64]{1,0:T(8,128)S(1)} %shard_map.55), channel_id=1, source_target_pairs={{0,8},{8,0},{16,24},{24,16},{1,9},{9,1},{17,25},{25,17},{2,10},{10... | collective-permute-start | bytes 49160 | tf_op jit(solution)/shard_map/ppermute | solution.py:38
  23.3 0.9 %collective-permute-done.6 = f32[64,64]{1,0:T(8,128)S(1)} collective-permute-done((f32[64,64]{1,0:T(8,128)S(1)}, f32[64,64]{1,0:T(8,128)S(1)}, u32[]{:S(2)}, u32[]{:S(2)}) %collective-permute-start.6) | collective-permute-done | bytes 16416 | tf_op jit(solution)/shard_map/ppermute | solution.py:38
  24.2 1.5 %collective-permute-start.7 = (f32[64,64]{1,0:T(8,128)S(1)}, f32[64,64]{1,0:T(8,128)S(1)}, u32[]{:S(2)}, u32[]{:S(2)}) collective-permute-start(f32[64,64]{1,0:T(8,128)S(1)} %add.13.inner_ref), channel_id=1, source_target_pairs={{0,16},{8,24},{16,0},{24,8},{1,17},{9,25},{17,1},{25,9},{2,18},{10... | collective-permute-start | bytes 49160 | tf_op jit(solution)/shard_map/ppermute | solution.py:38
  25.7 0.8 %shard_map.54 = (f32[1024,512]{1,0:T(8,128)S(1)}, f32[64,1024]{1,0:T(8,128)S(1)}) custom-call(s32[1]{0:T(128)} %bitcast.which_ref, f32[1024,512]{1,0:T(8,128)S(1)} %get-tuple-element.34.begun_ref, f32[64,512]{1,0:T(8,128)S(1)} %get-tuple-element.35.cols_ref, f32[64,64]{1,0:T(8,128)S(1)} %shard_map.52.inverse_ref, ...), custom_call_target="tpu_custom_call" | custom-call | flops 1073741824 | bytes 262144 | tf_op jit(solution)/shard_map/pallas_call | solution.py:268
  26.5 1.6 %collective-permute-done.7.other_ref = f32[64,64]{1,0:T(8,128)S(1)} collective-permute-done((f32[64,64]{1,0:T(8,128)S(1)}, f32[64,64]{1,0:T(8,128)S(1)}, u32[]{:S(2)}, u32[]{:S(2)}) %collective-permute-start.7) | collective-permute-done | bytes 16416 | tf_op jit(solution)/shard_map/ppermute | solution.py:38
  28.1 2.2 %shard_map.56 = (f32[1024,512]{1,0:T(8,128)}, f32[64,1024]{1,0:T(8,128)}) custom-call(f32[1024,512]{1,0:T(8,128)S(1)} %get-tuple-element.38.further_ref, f32[64,1024]{1,0:T(8,128)S(1)} %get-tuple-element.39.image_ref, bf16[192,1024]{1,0:T(8,128)(2,1)S(1)} %get-tuple-element.40.left_ref, f32[64,1024]{1,0:T(8,128)S(1)} %get-tuple-element.41.coeffs_ref, ...), custom_call_target="tpu_custom_call" | custom-call | flops 1073741824 | bytes 262144 | tf_op jit(solution)/shard_map/pallas_call | solution.py:268
  (3 shorter events, 0.0 us)
Async XLA Ops:
  3.3 2.5 %collective-permute-start = (f32[72,512]{1,0:T(8,128)S(1)}, f32[72,512]{1,0:T(8,128)S(1)}, u32[]{:S(2)}, u32[]{:S(2)}) collective-permute-start(f32[72,512]{1,0:T(8,128)S(1)} %shard_map.50), channel_id=1, source_target_pairs={{0,8},{8,0},{16,24},{24,16},{1,9},{9,1},{17,25},{25,17},{2,10},{10... | collective-permute-start | bytes 442376 | tf_op jit(solution)/shard_map/ppermute | solution.py:38
  3.8 4.0 %collective-permute-start.4 = (f32[64,512]{1,0:T(8,128)S(1)}, f32[64,512]{1,0:T(8,128)S(1)}, u32[]{:S(2)}, u32[]{:S(2)}) collective-permute-start(f32[64,512]{1,0:T(8,128)S(1)} %get-tuple-element.31.refs_3_), channel_id=1, source_target_pairs={{0,8},{9,1},{18,26},{27,19},{4,12},{13,5},{22,30},{31,23}} | collective-permute-start | bytes 393224 | tf_op jit(solution)/shard_map/ppermute | solution.py:53
  5.8 6.2 %collective-permute-start.1 = (f32[72,512]{1,0:T(8,128)S(1)}, f32[72,512]{1,0:T(8,128)S(1)}, u32[]{:S(2)}, u32[]{:S(2)}) collective-permute-start(f32[72,512]{1,0:T(8,128)S(1)} %add.11.mine_ref), channel_id=1, source_target_pairs={{0,16},{8,24},{16,0},{24,8},{1,17},{9,25},{17,1},{25,9},{2,18},{10... | collective-permute-start | bytes 442376 | tf_op jit(solution)/shard_map/ppermute | solution.py:38
  7.8 12.0 %collective-permute-start.5 = (f32[64,512]{1,0:T(8,128)S(1)}, f32[64,512]{1,0:T(8,128)S(1)}, u32[]{:S(2)}, u32[]{:S(2)}) collective-permute-start(f32[64,512]{1,0:T(8,128)S(1)} %broadcast_select_fusion.held_ref), channel_id=1, source_target_pairs={{0,16},{8,24},{9,25},{1,17},{18,2},{26,10},{27,11},{19,3},{4,20},{... | collective-permute-start | bytes 393224 | tf_op jit(solution)/shard_map/ppermute | solution.py:53
  12.1 9.1 %collective-permute-start.2 = (f32[64,512]{1,0:T(8,128)S(1)}, f32[64,512]{1,0:T(8,128)S(1)}, u32[]{:S(2)}, u32[]{:S(2)}) collective-permute-start(f32[64,512]{1,0:T(8,128)S(1)} %get-tuple-element.28.product_cols_ref), channel_id=1, source_target_pairs={{4,0},{12,1},{20,2},{28,3},{0,4},{8,5},{16,6},{24,7},{5,8},{13,9},... | collective-permute-start | bytes 393224 | tf_op jit(solution)/shard_map/ppermute | solution.py:71
  15.1 6.1 %collective-permute-start.3 = (f32[64,512]{1,0:T(8,128)S(1)}, f32[64,512]{1,0:T(8,128)S(1)}, u32[]{:S(2)}, u32[]{:S(2)}) collective-permute-start(f32[64,512]{1,0:T(8,128)S(1)} %get-tuple-element.28.product_cols_ref), channel_id=1, source_target_pairs={{16,0},{24,1},{0,2},{8,3},{20,4},{28,5},{4,6},{12,7},{17,8},{25,9}... | collective-permute-start | bytes 393224 | tf_op jit(solution)/shard_map/ppermute | solution.py:71
  21.6 2.6 %collective-permute-start.6 = (f32[64,64]{1,0:T(8,128)S(1)}, f32[64,64]{1,0:T(8,128)S(1)}, u32[]{:S(2)}, u32[]{:S(2)}) collective-permute-start(f32[64,64]{1,0:T(8,128)S(1)} %shard_map.55), channel_id=1, source_target_pairs={{0,8},{8,0},{16,24},{24,16},{1,9},{9,1},{17,25},{25,17},{2,10},{10... | collective-permute-start | bytes 49160 | tf_op jit(solution)/shard_map/ppermute | solution.py:38
  24.2 3.9 %collective-permute-start.7 = (f32[64,64]{1,0:T(8,128)S(1)}, f32[64,64]{1,0:T(8,128)S(1)}, u32[]{:S(2)}, u32[]{:S(2)}) collective-permute-start(f32[64,64]{1,0:T(8,128)S(1)} %add.13.inner_ref), channel_id=1, source_target_pairs={{0,16},{8,24},{16,0},{24,8},{1,17},{9,25},{17,1},{25,9},{2,18},{10... | collective-permute-start | bytes 49160 | tf_op jit(solution)/shard_map/ppermute | solution.py:38

commit v2 on v1

--- a/solution.py
+++ b/solution.py
@@ -36,6 +36,22 @@
 def partner(value, axis, step):
     size = lax.axis_size(axis)
     return lax.ppermute(value, axis, [(i, i ^ step) for i in range(size)])
+
+
+def tree_sum(parts):
+    while len(parts) > 1:
+        parts = [parts[i] + parts[i + 1] for i in range(0, len(parts), 2)]
+    return parts[0]
+
+
+def group_parts(value, axis, low, high):
+    parts = [value]
+    while low < high:
+        value = tree_sum(parts)
+        radix = min(4, high // low)
+        parts = [value] + [partner(value, axis, i * low) for i in range(1, radix)]
+        low *= radix
+    return parts
 
 
 def spread_rows(value, after):
@@ -83,12 +99,12 @@
     return copies
 
 
-def panel_kernel(ratio, which_ref, panel_ref, matrix_ref, *refs):
-    mine_refs, (held_ref, terms_ref, gram_ref, kept_ref, sems) = refs[:ratio], refs[ratio:]
-    width = panel_ref.shape[0]
-    pieces = sems.shape[0] // 2
+def product_kernel(ratio, which_ref, panel_ref, matrix_ref, *refs):
+    mine_refs, (out_ref, held_ref, kept_ref, sems) = refs[:ratio], refs[ratio:]
+    width, rows = panel_ref.shape
+    pieces = width // STRIP
     panel_copies = copy_rows(panel_ref, held_ref, sems, 0, pieces)
-    matrix_copies = copy_rows(matrix_ref, kept_ref, sems, pieces, pieces)
+    matrix_copies = copy_rows(matrix_ref, kept_ref, sems, pieces, sems.shape[0] - pieces)
     for copy in panel_copies:
         copy.wait()
     which = which_ref[0]
@@ -101,27 +117,21 @@
                 block = jnp.where(which == k, blocks[(k + shift) % ratio], block)
             mine_ref[:, j * width : (j + 1) * width] = block
     panel = held_ref[...]
-    terms_ref[...] = jnp.concatenate(split(panel, 3), axis=0)
-    to_strip(dot(panel, panel, ((1,), (1,))), gram_ref)
-    for copy in matrix_copies:
-        copy.wait()
-
-
-def product_kernel(terms_ref, matrix_ref, gram_ref, out_ref):
-    width = out_ref.shape[0] - STRIP
-    rows = matrix_ref.shape[0]
+    to_strip(dot(panel, panel, ((1,), (1,))), out_ref.at[width:, :])
     chunk = 256
+    each = len(matrix_copies) * chunk // rows
     total = jnp.zeros((width, matrix_ref.shape[1]), jnp.float32)
     for start in range(0, rows, chunk):
+        for copy in matrix_copies[start // chunk * each : (start // chunk + 1) * each]:
+            copy.wait()
         span = slice(start, start + chunk)
-        parts = split(matrix_ref[span, :], 3)
-        for i, part in enumerate(parts):
+        terms = jnp.concatenate(split(held_ref[:, span], 3), axis=0)
+        for i, part in enumerate(split(kept_ref[span, :], 3)):
             count = 3 - i
-            out = dot16(terms_ref[: count * width, span], part, ((1,), (0,)))
+            out = dot16(terms[: count * width, :], part, ((1,), (0,)))
             for t in range(count):
                 total = total + out[t * width : (t + 1) * width, :]
     out_ref[:width, :] = total
-    out_ref[width:, :] = gram_ref[...]
 
 
 def to_strip(value, strip_ref):
@@ -235,11 +245,11 @@
 
 
 def update_kernel(
-    further_ref, image_ref, left_ref, coeffs_ref, coeffs_cols_ref, inverse_ref,
-    inner_ref, other_ref, updated_ref, w_ref, buffer_ref, w_buffer_ref, sems,
+    further_ref, image_ref, left_ref, coeffs_ref, coeffs_cols_ref, inverse_ref, *refs
 ):
+    inners, (updated_ref, w_ref, buffer_ref, w_buffer_ref, sems) = refs[:-5], refs[-5:]
     inverse = inverse_ref[...]
-    inner = inner_ref[...] + other_ref[...]
+    inner = tree_sum([part[...] for part in inners])
     right = dot(inverse, dot(inner, coeffs_cols_ref[...], ((1,), (0,))), ((1,), (0,)))
     right = stack_right(4.0 * right)
     count = sems.shape[0] - 1
@@ -284,13 +294,12 @@
     which = (lax.axis_index("col") // n_row).astype(jnp.int32).reshape(1)
     chunks = 8
 
-    *mines, panel_t, terms, gram, kept = call(
-        functools.partial(panel_kernel, ratio),
+    *mines, message, panel_t, kept = call(
+        functools.partial(product_kernel, ratio),
         (
             *[shape(width, cols)] * ratio,
+            shape(width + STRIP, cols),
             shape(width, rows),
-            shape(3 * width, rows, dtype=jnp.bfloat16),
-            shape(STRIP, cols),
             shape(rows, cols),
         ),
         (
@@ -299,11 +308,8 @@
             pltpu.with_memory_space_constraint(matrix, pltpu.HBM),
         ),
         in_specs=[SMEM, HBM, HBM],
-        scratch=[pltpu.SemaphoreType.DMA((2 * chunks,))],
-        flops=1 << 28,
-    )
-    message = call(
-        product_kernel, shape(width + STRIP, cols), (terms, kept, gram), flops=1 << 30
+        scratch=[pltpu.SemaphoreType.DMA((width // STRIP + 2 * chunks,))],
+        flops=1 << 30,
     )
     step = 1
     while 2 * step < n_row:
@@ -339,17 +345,11 @@
         in_specs=[SMEM] + [VMEM] * (3 + ratio),
         flops=1 << 30,
     )
-    step = 1
-    while 2 * step < n_row:
-        inner = inner + partner(inner, "row", step)
-        step *= 2
+    inners = group_parts(inner, "row", 1, n_row)[::-1]
     updated, w_rows = call(
         update_kernel,
         (shape(rows, cols), shape(width, rows)),
-        (
-            further, image, left, coeffs, coeffs_cols, inverse,
-            inner, partner(inner, "row", step),
-        ),
+        (further, image, left, coeffs, coeffs_cols, inverse, *inners),
         out_specs=(HBM, HBM),
         scratch=[
             pltpu.VMEM((rows, cols), jnp.float32),

time: 30.5 us -> 31 us (1.016)
  Pallas kernels: 10.2 us -> 10.6 us
    pallas_call x8 -> x7, Pallas kernels: 10.2 us -> 10.6 us  [call(): pl.pallas_call(kernel, out_shape=outs, in_specs=in_specs or [VMEM] * len(...]
    ppermute x4 -> x5, starting transfers between devices: 5.68 us -> 5.83 us  [partner(): return lax.ppermute(value, axis, [(i, i ^ step) for i in range(size)])]
    ppermute x4 -> x5, waiting for transfers between devices: 4.63 us -> 4.71 us  [partner(): return lax.ppermute(value, axis, [(i, i ^ step) for i in range(size)])]
  transfers between devices with their start and end apart: 8 -> 9, of which waited for: 3 -> 3; matrix products, arithmetic and copies ran while one was open for 0% -> 0% of each run, Pallas kernels for 17% -> 16%
where the time goes in v2:
time: 31 us; the launch traced here: 30.8 us
  starting transfers between devices  14.7 us (47%)
  Pallas kernels  10.6 us (34%)
  waiting for transfers between devices  4.72 us (15%)
  between operations  0.76 us (2%)
    pallas_call x7, Pallas kernels, call(): pl.pallas_call(kernel, out_shape=outs, in_specs=in_specs or [VMEM] * len(...  10.6 us
    ppermute x5, starting transfers between devices, partner(): return lax.ppermute(value, axis, [(i, i ^ step) for i in range(size)])  5.83 us
    ppermute x2, starting transfers between devices, transpose_grid(): return lax.ppermute(value, ('row', 'col'), pairs)  4.91 us
    ppermute x5, waiting for transfers between devices, partner(): return lax.ppermute(value, axis, [(i, i ^ step) for i in range(size)])  4.71 us
    ppermute x2, starting transfers between devices, spread_rows(): received = lax.ppermute(value, ('row', 'col'), pairs)  4.01 us
  transfers between devices with their start and end apart: 9, of which 3 were waited for; matrix products, arithmetic and copies ran while one was open for 0% of the time, Pallas kernels for 16%

profile of v2, /device:TPU:0, one launch (start us, length us, event | category | flops | bytes accessed | tf_op | source)
XLA Modules:
  0.0 30.8 jit_solution(15318305025817939942)
XLA Ops:
  0.6 2.9 %shard_map.49 = (f32[64,512]{1,0:T(8,128)S(1)}, f32[64,512]{1,0:T(8,128)S(1)}, f32[72,512]{1,0:T(8,128)S(1)}, f32[64,1024]{1,0:T(8,128)S(1)}, f32[1024,512]{1,0:T(8,128)S(1)}) custom-call(s32[1]{0:T(128)} %bitcast.which_ref, f32[64,1024]{1,0:T(8,128)} %bitcast.5, f32[1024,512]{1,0:T(8,128)} %matrix_ref.1), custom_call_target="tpu_custom_call" | custom-call | flops 1073741824 | bytes 262144 | tf_op jit(solution)/shard_map/pallas_call | solution.py:278
  3.6 0.5 %collective-permute-start = (f32[72,512]{1,0:T(8,128)S(1)}, f32[72,512]{1,0:T(8,128)S(1)}, u32[]{:S(2)}, u32[]{:S(2)}) collective-permute-start(f32[72,512]{1,0:T(8,128)S(1)} %get-tuple-element.24), channel_id=1, source_target_pairs={{0,8},{8,0},{16,24},{24,16},{1,9},{9,1},{17,25},{25,17},{2,10},{10... | collective-permute-start | bytes 442376 | tf_op jit(solution)/shard_map/ppermute | solution.py:38
  4.1 2.0 %collective-permute-start.4 = (f32[64,512]{1,0:T(8,128)S(1)}, f32[64,512]{1,0:T(8,128)S(1)}, u32[]{:S(2)}, u32[]{:S(2)}) collective-permute-start(f32[64,512]{1,0:T(8,128)S(1)} %get-tuple-element.29.refs_3_), channel_id=1, source_target_pairs={{0,8},{9,1},{18,26},{27,19},{4,12},{13,5},{22,30},{31,23}} | collective-permute-start | bytes 393224 | tf_op jit(solution)/shard_map/ppermute | solution.py:69
  6.1 0.0 collective-permute-done
  6.1 2.0 %collective-permute-start.1 = (f32[72,512]{1,0:T(8,128)S(1)}, f32[72,512]{1,0:T(8,128)S(1)}, u32[]{:S(2)}, u32[]{:S(2)}) collective-permute-start(f32[72,512]{1,0:T(8,128)S(1)} %add.8.mine_ref), channel_id=1, source_target_pairs={{0,16},{8,24},{16,0},{24,8},{1,17},{9,25},{17,1},{25,9},{2,18},{10... | collective-permute-start | bytes 442376 | tf_op jit(solution)/shard_map/ppermute | solution.py:38
  8.1 0.0 collective-permute-done.4
  8.1 2.0 %collective-permute-start.5 = (f32[64,512]{1,0:T(8,128)S(1)}, f32[64,512]{1,0:T(8,128)S(1)}, u32[]{:S(2)}, u32[]{:S(2)}) collective-permute-start(f32[64,512]{1,0:T(8,128)S(1)} %broadcast_select_fusion.held_ref), channel_id=1, source_target_pairs={{0,16},{8,24},{9,25},{1,17},{18,2},{26,10},{27,11},{19,3},{4,20},{... | collective-permute-start | bytes 393224 | tf_op jit(solution)/shard_map/ppermute | solution.py:69
  10.2 2.1 %collective-permute-done.1.other_ref = f32[72,512]{1,0:T(8,128)S(1)} collective-permute-done((f32[72,512]{1,0:T(8,128)S(1)}, f32[72,512]{1,0:T(8,128)S(1)}, u32[]{:S(2)}, u32[]{:S(2)}) %collective-permute-start.1) | collective-permute-done | bytes 147488 | tf_op jit(solution)/shard_map/ppermute | solution.py:38
  12.3 0.1 shard_map.50
  12.4 3.1 %collective-permute-start.2 = (f32[64,512]{1,0:T(8,128)S(1)}, f32[64,512]{1,0:T(8,128)S(1)}, u32[]{:S(2)}, u32[]{:S(2)}) collective-permute-start(f32[64,512]{1,0:T(8,128)S(1)} %get-tuple-element.25.product_cols_ref), channel_id=1, source_target_pairs={{4,0},{12,1},{20,2},{28,3},{0,4},{8,5},{16,6},{24,7},{5,8},{13,9},... | collective-permute-start | bytes 393224 | tf_op jit(solution)/shard_map/ppermute | solution.py:87
  15.5 1.8 %collective-permute-start.3 = (f32[64,512]{1,0:T(8,128)S(1)}, f32[64,512]{1,0:T(8,128)S(1)}, u32[]{:S(2)}, u32[]{:S(2)}) collective-permute-start(f32[64,512]{1,0:T(8,128)S(1)} %get-tuple-element.25.product_cols_ref), channel_id=1, source_target_pairs={{16,0},{24,1},{0,2},{8,3},{20,4},{28,5},{4,6},{12,7},{17,8},{25,9}... | collective-permute-start | bytes 393224 | tf_op jit(solution)/shard_map/ppermute | solution.py:87
  17.3 2.8 %shard_map.51.inverse_ref = f32[64,64]{1,0:T(8,128)S(1)} custom-call(f32[64,64]{1,0:T(8,128)S(1)} %get-tuple-element.28.gram_ref), custom_call_target="tpu_custom_call" | custom-call | flops 1073741824 | bytes 262144 | tf_op jit(solution)/shard_map/pallas_call | solution.py:278
  20.1 0.0 collective-permute-done.5.received_ref
  20.1 1.4 %shard_map.52 = (f32[1024,512]{1,0:T(8,128)S(1)}, f32[64,1024]{1,0:T(8,128)}, bf16[192,1024]{1,0:T(8,128)(2,1)S(1)}, f32[64,1024]{1,0:T(8,128)S(1)}, f32[64,512]{1,0:T(8,128)S(1)}, /*index=5*/f32[64,512]{1,0:T(8,128)S(1)}) custom-call(f32[1024,512]{1,0:T(8,128)S(1)} %get-tuple-element.26.matrix_ref, f32[64,1024]{1,0:T(8,128)S(1)} %get-tuple-element.27.panel_ref, ...), custom_call_target="tpu_custom_call" | custom-call | flops 1073741824 | bytes 262144 | tf_op jit(solution)/shard_map/pallas_call | solution.py:278
  21.5 0.0 collective-permute-done.2.refs_0_
  21.5 0.0 collective-permute-done.3.refs_1_
  21.5 0.4 %shard_map.54.refs_3_ = f32[64,64]{1,0:T(8,128)S(1)} custom-call(f32[64,512]{1,0:T(8,128)S(1)} %collective-permute-done.2.refs_0_, f32[64,512]{1,0:T(8,128)S(1)} %collective-permute-done.3.refs_1_, f32[64,512]{1,0:T(8,128)S(1)} %get-tuple-element.41.refs_2_, f32[64,512]{1,0:T(8,128)S(1)} %get-tuple-element.29.refs_3_), custom_call_target="tpu_custom_call" | custom-call | flops 16777216 | bytes 262144 | tf_op jit(solution)/shard_map/pallas_call | solution.py:278
  21.9 2.8 %collective-permute-start.6 = (f32[64,64]{1,0:T(8,128)S(1)}, f32[64,64]{1,0:T(8,128)S(1)}, u32[]{:S(2)}, u32[]{:S(2)}) collective-permute-start(f32[64,64]{1,0:T(8,128)S(1)} %shard_map.54.refs_3_), channel_id=1, source_target_pairs={{0,24},{8,16},{16,8},{24,0},{1,25},{9,17},{17,9},{25,1},{2,26},{10... | collective-permute-start | bytes 49160 | tf_op jit(solution)/shard_map/ppermute | solution.py:38
  24.7 0.5 %collective-permute-start.7 = (f32[64,64]{1,0:T(8,128)S(1)}, f32[64,64]{1,0:T(8,128)S(1)}, u32[]{:S(2)}, u32[]{:S(2)}) collective-permute-start(f32[64,64]{1,0:T(8,128)S(1)} %shard_map.54.refs_3_), channel_id=1, source_target_pairs={{0,16},{8,24},{16,0},{24,8},{1,17},{9,25},{17,1},{25,9},{2,18},{10... | collective-permute-start | bytes 49160 | tf_op jit(solution)/shard_map/ppermute | solution.py:38
  25.3 0.8 %shard_map.53 = (f32[1024,512]{1,0:T(8,128)S(1)}, f32[64,1024]{1,0:T(8,128)S(1)}) custom-call(s32[1]{0:T(128)} %bitcast.which_ref, f32[1024,512]{1,0:T(8,128)S(1)} %get-tuple-element.32.begun_ref, f32[64,512]{1,0:T(8,128)S(1)} %get-tuple-element.33.cols_ref, f32[64,64]{1,0:T(8,128)S(1)} %shard_map.51.inverse_ref, ...), custom_call_target="tpu_custom_call" | custom-call | flops 1073741824 | bytes 262144 | tf_op jit(solution)/shard_map/pallas_call | solution.py:278
  26.1 0.3 collective-permute-done.6.refs_0_
  26.3 2.3 %collective-permute-done.7.refs_1_ = f32[64,64]{1,0:T(8,128)S(1)} collective-permute-done((f32[64,64]{1,0:T(8,128)S(1)}, f32[64,64]{1,0:T(8,128)S(1)}, u32[]{:S(2)}, u32[]{:S(2)}) %collective-permute-start.7) | collective-permute-done | bytes 16416 | tf_op jit(solution)/shard_map/ppermute | solution.py:38
  28.6 0.0 collective-permute-done.8.refs_2_
  28.6 2.2 %shard_map.55 = (f32[1024,512]{1,0:T(8,128)}, f32[64,1024]{1,0:T(8,128)}) custom-call(f32[1024,512]{1,0:T(8,128)S(1)} %get-tuple-element.36.further_ref, f32[64,1024]{1,0:T(8,128)S(1)} %get-tuple-element.37.image_ref, bf16[192,1024]{1,0:T(8,128)(2,1)S(1)} %get-tuple-element.38.left_ref, f32[64,1024]{1,0:T(8,128)S(1)} %get-tuple-element.39.coeffs_ref, ...), custom_call_target="tpu_custom_call" | custom-call | flops 1073741824 | bytes 262144 | tf_op jit(solution)/shard_map/pallas_call | solution.py:278
  (3 shorter events, 0.0 us)
Async XLA Ops:
  3.6 2.5 %collective-permute-start = (f32[72,512]{1,0:T(8,128)S(1)}, f32[72,512]{1,0:T(8,128)S(1)}, u32[]{:S(2)}, u32[]{:S(2)}) collective-permute-start(f32[72,512]{1,0:T(8,128)S(1)} %get-tuple-element.24), channel_id=1, source_target_pairs={{0,8},{8,0},{16,24},{24,16},{1,9},{9,1},{17,25},{25,17},{2,10},{10... | collective-permute-start | bytes 442376 | tf_op jit(solution)/shard_map/ppermute | solution.py:38
  4.1 4.0 %collective-permute-start.4 = (f32[64,512]{1,0:T(8,128)S(1)}, f32[64,512]{1,0:T(8,128)S(1)}, u32[]{:S(2)}, u32[]{:S(2)}) collective-permute-start(f32[64,512]{1,0:T(8,128)S(1)} %get-tuple-element.29.refs_3_), channel_id=1, source_target_pairs={{0,8},{9,1},{18,26},{27,19},{4,12},{13,5},{22,30},{31,23}} | collective-permute-start | bytes 393224 | tf_op jit(solution)/shard_map/ppermute | solution.py:69
  6.1 6.2 %collective-permute-start.1 = (f32[72,512]{1,0:T(8,128)S(1)}, f32[72,512]{1,0:T(8,128)S(1)}, u32[]{:S(2)}, u32[]{:S(2)}) collective-permute-start(f32[72,512]{1,0:T(8,128)S(1)} %add.8.mine_ref), channel_id=1, source_target_pairs={{0,16},{8,24},{16,0},{24,8},{1,17},{9,25},{17,1},{25,9},{2,18},{10... | collective-permute-start | bytes 442376 | tf_op jit(solution)/shard_map/ppermute | solution.py:38
  8.1 12.0 %collective-permute-start.5 = (f32[64,512]{1,0:T(8,128)S(1)}, f32[64,512]{1,0:T(8,128)S(1)}, u32[]{:S(2)}, u32[]{:S(2)}) collective-permute-start(f32[64,512]{1,0:T(8,128)S(1)} %broadcast_select_fusion.held_ref), channel_id=1, source_target_pairs={{0,16},{8,24},{9,25},{1,17},{18,2},{26,10},{27,11},{19,3},{4,20},{... | collective-permute-start | bytes 393224 | tf_op jit(solution)/shard_map/ppermute | solution.py:69
  12.4 9.1 %collective-permute-start.2 = (f32[64,512]{1,0:T(8,128)S(1)}, f32[64,512]{1,0:T(8,128)S(1)}, u32[]{:S(2)}, u32[]{:S(2)}) collective-permute-start(f32[64,512]{1,0:T(8,128)S(1)} %get-tuple-element.25.product_cols_ref), channel_id=1, source_target_pairs={{4,0},{12,1},{20,2},{28,3},{0,4},{8,5},{16,6},{24,7},{5,8},{13,9},... | collective-permute-start | bytes 393224 | tf_op jit(solution)/shard_map/ppermute | solution.py:87
  15.5 6.1 %collective-permute-start.3 = (f32[64,512]{1,0:T(8,128)S(1)}, f32[64,512]{1,0:T(8,128)S(1)}, u32[]{:S(2)}, u32[]{:S(2)}) collective-permute-start(f32[64,512]{1,0:T(8,128)S(1)} %get-tuple-element.25.product_cols_ref), channel_id=1, source_target_pairs={{16,0},{24,1},{0,2},{8,3},{20,4},{28,5},{4,6},{12,7},{17,8},{25,9}... | collective-permute-start | bytes 393224 | tf_op jit(solution)/shard_map/ppermute | solution.py:87
  21.9 4.4 %collective-permute-start.6 = (f32[64,64]{1,0:T(8,128)S(1)}, f32[64,64]{1,0:T(8,128)S(1)}, u32[]{:S(2)}, u32[]{:S(2)}) collective-permute-start(f32[64,64]{1,0:T(8,128)S(1)} %shard_map.54.refs_3_), channel_id=1, source_target_pairs={{0,24},{8,16},{16,8},{24,0},{1,25},{9,17},{17,9},{25,1},{2,26},{10... | collective-permute-start | bytes 49160 | tf_op jit(solution)/shard_map/ppermute | solution.py:38
  24.7 3.9 %collective-permute-start.7 = (f32[64,64]{1,0:T(8,128)S(1)}, f32[64,64]{1,0:T(8,128)S(1)}, u32[]{:S(2)}, u32[]{:S(2)}) collective-permute-start(f32[64,64]{1,0:T(8,128)S(1)} %shard_map.54.refs_3_), channel_id=1, source_target_pairs={{0,16},{8,24},{16,0},{24,8},{1,17},{9,25},{17,1},{25,9},{2,18},{10... | collective-permute-start | bytes 49160 | tf_op jit(solution)/shard_map/ppermute | solution.py:38
  25.3 3.4 %collective-permute-start.8 = (f32[64,64]{1,0:T(8,128)S(1)}, f32[64,64]{1,0:T(8,128)S(1)}, u32[]{:S(2)}, u32[]{:S(2)}) collective-permute-start(f32[64,64]{1,0:T(8,128)S(1)} %shard_map.54.refs_3_), channel_id=1, source_target_pairs={{0,8},{8,0},{16,24},{24,16},{1,9},{9,1},{17,25},{25,17},{2,10},{10... | collective-permute-start | bytes 49160 | tf_op jit(solution)/shard_map/ppermute | solution.py:38

commit v3 on v1

--- a/solution.py
+++ b/solution.py
@@ -36,6 +36,22 @@
 def partner(value, axis, step):
     size = lax.axis_size(axis)
     return lax.ppermute(value, axis, [(i, i ^ step) for i in range(size)])
+
+
+def tree_sum(parts):
+    while len(parts) > 1:
+        parts = [parts[i] + parts[i + 1] for i in range(0, len(parts), 2)]
+    return parts[0]
+
+
+def group_parts(value, axis, low, high):
+    parts = [value]
+    while low < high:
+        value = tree_sum(parts)
+        radix = min(4, high // low)
+        parts = [value] + [partner(value, axis, i * low) for i in range(1, radix)]
+        low *= radix
+    return parts
 
 
 def spread_rows(value, after):
@@ -84,7 +100,8 @@
 
 
 def panel_kernel(ratio, which_ref, panel_ref, matrix_ref, *refs):
-    mine_refs, (held_ref, terms_ref, gram_ref, kept_ref, sems) = refs[:ratio], refs[ratio:]
+    block_refs, refs = refs[:ratio], refs[ratio:]
+    mine_ref, held_ref, terms_ref, gram_ref, kept_ref, sems = refs
     width = panel_ref.shape[0]
     pieces = sems.shape[0] // 2
     panel_copies = copy_rows(panel_ref, held_ref, sems, 0, pieces)
@@ -92,19 +109,34 @@
     for copy in panel_copies:
         copy.wait()
     which = which_ref[0]
-    for j in range(mine_refs[0].shape[1] // width):
+    halves = [[] for _ in range(ratio)]
+    for j in range(mine_ref.shape[1] // width):
         start = j * ratio * width
         blocks = [held_ref[:, start + k * width : start + (k + 1) * width] for k in range(ratio)]
-        for shift, mine_ref in enumerate(mine_refs):
+        for shift in range(ratio):
             block = blocks[shift]
             for k in range(1, ratio):
                 block = jnp.where(which == k, blocks[(k + shift) % ratio], block)
-            mine_ref[:, j * width : (j + 1) * width] = block
+            halves[shift].append(block)
+    halves = [jnp.concatenate(half, axis=1) for half in halves]
+    mine_ref[...] = halves[0]
+    for half, block_ref in zip(halves, block_refs):
+        block_ref[...] = jnp.concatenate(split(half, 3), axis=0)
     panel = held_ref[...]
     terms_ref[...] = jnp.concatenate(split(panel, 3), axis=0)
     to_strip(dot(panel, panel, ((1,), (1,))), gram_ref)
     for copy in matrix_copies:
         copy.wait()
+
+
+def exact_product(terms, value, contract):
+    width = terms.shape[0] // 3
+    total = 0.0
+    for i, part in enumerate(split(value, 3)):
+        out = dot16(terms[: (3 - i) * width, :], part, contract)
+        for t in range(3 - i):
+            total = total + out[t * width : (t + 1) * width, :]
+    return total
 
 
 def product_kernel(terms_ref, matrix_ref, gram_ref, out_ref):
@@ -114,12 +146,7 @@
     total = jnp.zeros((width, matrix_ref.shape[1]), jnp.float32)
     for start in range(0, rows, chunk):
         span = slice(start, start + chunk)
-        parts = split(matrix_ref[span, :], 3)
-        for i, part in enumerate(parts):
-            count = 3 - i
-            out = dot16(terms_ref[: count * width, span], part, ((1,), (0,)))
-            for t in range(count):
-                total = total + out[t * width : (t + 1) * width, :]
+        total = total + exact_product(terms_ref[:, span], matrix_ref[span, :], ((1,), (0,)))
     out_ref[:width, :] = total
     out_ref[width:, :] = gram_ref[...]
 
@@ -206,10 +233,10 @@
 
 def inner_kernel(*refs):
     count = len(refs) // 2
-    inner_ref = refs[-1]
-    inner_ref[...] = sum(
-        dot(refs[count + i][...], refs[i][...], ((1,), (1,))) for i in range(count)
-    )
+    total = 0.0
+    for half_ref, block_ref in zip(refs[:count], refs[count:-1]):
+        total = total + exact_product(block_ref[...], half_ref[...], ((1,), (1,)))
+    refs[-1][...] = total
 
 
 def image_kernel(ratio, which_ref, begun_ref, cols_ref, inverse_ref, *refs):
@@ -235,11 +262,11 @@
 
 
 def update_kernel(
-    further_ref, image_ref, left_ref, coeffs_ref, coeffs_cols_ref, inverse_ref,
-    inner_ref, other_ref, updated_ref, w_ref, buffer_ref, w_buffer_ref, sems,
+    further_ref, image_ref, left_ref, coeffs_ref, coeffs_cols_ref, inverse_ref, *refs
 ):
+    inners, (updated_ref, w_ref, buffer_ref, w_buffer_ref, sems) = refs[:-5], refs[-5:]
     inverse = inverse_ref[...]
-    inner = inner_ref[...] + other_ref[...]
+    inner = tree_sum([part[...] for part in inners])
     right = dot(inverse, dot(inner, coeffs_cols_ref[...], ((1,), (0,))), ((1,), (0,)))
     right = stack_right(4.0 * right)
     count = sems.shape[0] - 1
@@ -284,10 +311,11 @@
     which = (lax.axis_index("col") // n_row).astype(jnp.int32).reshape(1)
     chunks = 8
 
-    *mines, panel_t, terms, gram, kept = call(
+    *blocks, mine, panel_t, terms, gram, kept = call(
         functools.partial(panel_kernel, ratio),
         (
-            *[shape(width, cols)] * ratio,
+            *[shape(3 * width, cols, dtype=jnp.bfloat16)] * ratio,
+            shape(width, cols),
             shape(width, rows),
             shape(3 * width, rows, dtype=jnp.bfloat16),
             shape(STRIP, cols),
@@ -310,7 +338,7 @@
         message = message + partner(message, "row", step)
         step *= 2
     last = partner(message, "row", step)
-    held, received, takes = spread_rows(mines[0], message)
+    held, received, takes = spread_rows(mine, message)
     product_cols, gram = call(
         finish_kernel, (shape(width, cols), shape(width, width)), (last, message), flops=1 << 24
     )
@@ -331,7 +359,7 @@
         flops=1 << 30,
     )
     halves, begun = lax.optimization_barrier((halves, begun))
-    inner = call(inner_kernel, shape(width, width), (*halves, *mines[::-1]), flops=1 << 24)
+    inner = call(inner_kernel, shape(width, width), (*halves, *blocks[::-1]), flops=1 << 24)
     further, image = call(
         functools.partial(image_kernel, ratio),
         (shape(rows, cols), shape(width, rows)),
@@ -339,17 +367,11 @@
         in_specs=[SMEM] + [VMEM] * (3 + ratio),
         flops=1 << 30,
     )
-    step = 1
-    while 2 * step < n_row:
-        inner = inner + partner(inner, "row", step)
-        step *= 2
+    inners = group_parts(inner, "row", 1, n_row)[::-1]
     updated, w_rows = call(
         update_kernel,
         (shape(rows, cols), shape(width, rows)),
-        (
-            further, image, left, coeffs, coeffs_cols, inverse,
-            inner, partner(inner, "row", step),
-        ),
+        (further, image, left, coeffs, coeffs_cols, inverse, *inners),
         out_specs=(HBM, HBM),
         scratch=[
             pltpu.VMEM((rows, cols), jnp.float32),

time: 30.5 us -> 30.3 us (level)
  starting transfers between devices: 14.6 us -> 13.4 us
  waiting for transfers between devices: 4.65 us -> 5.72 us
    ppermute x4 -> x5, starting transfers between devices: 5.68 us -> 3.78 us  [partner(): return lax.ppermute(value, axis, [(i, i ^ step) for i in range(size)])]
    ppermute x2, waiting for transfers between devices: 0.01 us -> 1.87 us  [transpose_grid(): return lax.ppermute(value, ('row', 'col'), pairs)]
    ppermute x2, starting transfers between devices: 4.01 us -> 5.28 us  [spread_rows(): received = lax.ppermute(value, ('row', 'col'), pairs)]
    ppermute x4 -> x5, waiting for transfers between devices: 4.63 us -> 3.85 us  [partner(): return lax.ppermute(value, axis, [(i, i ^ step) for i in range(size)])]
    ppermute x2, starting transfers between devices: 4.91 us -> 4.37 us  [transpose_grid(): return lax.ppermute(value, ('row', 'col'), pairs)]
  transfers between devices with their start and end apart: 8 -> 9, of which waited for: 3 -> 4; matrix products, arithmetic and copies ran while one was open for 0% -> 0% of each run, Pallas kernels for 17% -> 17%
where the time goes in v3:
time: 30.3 us; the launch traced here: 30.2 us
  starting transfers between devices  13.4 us (44%)
  Pallas kernels  10.2 us (34%)
  waiting for transfers between devices  5.72 us (19%)
  between operations  0.72 us (2%)
    pallas_call x8, Pallas kernels, call(): pl.pallas_call(kernel, out_shape=outs, in_specs=in_specs or [VMEM] * len(...  10.2 us
    ppermute x2, starting transfers between devices, spread_rows(): received = lax.ppermute(value, ('row', 'col'), pairs)  5.28 us
    ppermute x2, starting transfers between devices, transpose_grid(): return lax.ppermute(value, ('row', 'col'), pairs)  4.37 us
    ppermute x5, waiting for transfers between devices, partner(): return lax.ppermute(value, axis, [(i, i ^ step) for i in range(size)])  3.85 us
    ppermute x5, starting transfers between devices, partner(): return lax.ppermute(value, axis, [(i, i ^ step) for i in range(size)])  3.78 us
    ppermute x2, waiting for transfers between devices, transpose_grid(): return lax.ppermute(value, ('row', 'col'), pairs)  1.87 us
  transfers between devices with their start and end apart: 9, of which 4 were waited for; matrix products, arithmetic and copies ran while one was open for 0% of the time, Pallas kernels for 17%

profile of v3, /device:TPU:0, one launch (start us, length us, event | category | flops | bytes accessed | tf_op | source)
XLA Modules:
  0.0 30.2 jit_solution(5812769047314213423)
XLA Ops:
  0.6 1.8 %shard_map.49 = (bf16[192,512]{1,0:T(8,128)(2,1)S(1)}, bf16[192,512]{1,0:T(8,128)(2,1)S(1)}, f32[64,512]{1,0:T(8,128)S(1)}, f32[64,1024]{1,0:T(8,128)S(1)}, bf16...) custom-call(s32[1]{0:T(128)} %bitcast.which_ref, f32[64,1024]{1,0:T(8,128)} %bitcast.5, ...), custom_call_target="tpu_custom_call" | custom-call | flops 268435456 | bytes 262144 | tf_op jit(solution)/shard_map/pallas_call | solution.py:295
  2.5 0.8 %shard_map.50 = f32[72,512]{1,0:T(8,128)S(1)} custom-call(bf16[192,1024]{1,0:T(8,128)(2,1)S(1)} %get-tuple-element.26.terms_ref, f32[1024,512]{1,0:T(8,128)S(1)} %get-tuple-element.27.matrix_ref, f32[8,512]{1,0:T(8,128)S(1)} %get-tuple-element.28.gram_ref), custom_call_target="tpu_custom_call" | custom-call | flops 1073741824 | bytes 262144 | tf_op jit(solution)/shard_map/pallas_call | solution.py:295
  3.3 0.5 %collective-permute-start = (f32[72,512]{1,0:T(8,128)S(1)}, f32[72,512]{1,0:T(8,128)S(1)}, u32[]{:S(2)}, u32[]{:S(2)}) collective-permute-start(f32[72,512]{1,0:T(8,128)S(1)} %shard_map.50), channel_id=1, source_target_pairs={{0,8},{8,0},{16,24},{24,16},{1,9},{9,1},{17,25},{25,17},{2,10},{10... | collective-permute-start | bytes 442376 | tf_op jit(solution)/shard_map/ppermute | solution.py:38
  3.8 2.6 %collective-permute-start.4 = (f32[64,512]{1,0:T(8,128)S(1)}, f32[64,512]{1,0:T(8,128)}, u32[]{:S(2)}, u32[]{:S(2)}) collective-permute-start(f32[64,512]{1,0:T(8,128)S(1)} %get-tuple-element.32), channel_id=1, source_target_pairs={{0,8},{9,1},{18,26},{27,19},{4,12},{13,5},{22,30},{31,23}} | collective-permute-start | bytes 393224 | tf_op jit(solution)/shard_map/ppermute | solution.py:69
  6.4 0.0 collective-permute-done
  6.4 1.3 %collective-permute-start.1 = (f32[72,512]{1,0:T(8,128)S(1)}, f32[72,512]{1,0:T(8,128)S(1)}, u32[]{:S(2)}, u32[]{:S(2)}) collective-permute-start(f32[72,512]{1,0:T(8,128)S(1)} %add.8.mine_ref), channel_id=1, source_target_pairs={{0,16},{8,24},{16,0},{24,8},{1,17},{9,25},{17,1},{25,9},{2,18},{10... | collective-permute-start | bytes 442376 | tf_op jit(solution)/shard_map/ppermute | solution.py:38
  7.8 2.7 %collective-permute-start.5 = (f32[64,512]{1,0:T(8,128)S(1)}, f32[64,512]{1,0:T(8,128)S(1)}, u32[]{:S(2)}, u32[]{:S(2)}) collective-permute-start(f32[64,512]{1,0:T(8,128)S(1)} %broadcast_select_fusion.held_ref), channel_id=1, source_target_pairs={{0,16},{8,24},{9,25},{1,17},{18,2},{26,10},{27,11},{19,3},{4,20},{... | collective-permute-start | bytes 393224 | tf_op jit(solution)/shard_map/ppermute | solution.py:69
  10.5 1.8 %collective-permute-done.1.other_ref = f32[72,512]{1,0:T(8,128)S(1)} collective-permute-done((f32[72,512]{1,0:T(8,128)S(1)}, f32[72,512]{1,0:T(8,128)S(1)}, u32[]{:S(2)}, u32[]{:S(2)}) %collective-permute-start.1) | collective-permute-done | bytes 147488 | tf_op jit(solution)/shard_map/ppermute | solution.py:38
  12.2 0.1 shard_map.51
  12.3 3.4 %collective-permute-start.2 = (f32[64,512]{1,0:T(8,128)S(1)}, f32[64,512]{1,0:T(8,128)S(1)}, u32[]{:S(2)}, u32[]{:S(2)}) collective-permute-start(f32[64,512]{1,0:T(8,128)S(1)} %get-tuple-element.29.product_cols_ref), channel_id=1, source_target_pairs={{4,0},{12,1},{20,2},{28,3},{0,4},{8,5},{16,6},{24,7},{5,8},{13,9},... | collective-permute-start | bytes 393224 | tf_op jit(solution)/shard_map/ppermute | solution.py:87
  15.8 0.9 %collective-permute-start.3 = (f32[64,512]{1,0:T(8,128)S(1)}, f32[64,512]{1,0:T(8,128)S(1)}, u32[]{:S(2)}, u32[]{:S(2)}) collective-permute-start(f32[64,512]{1,0:T(8,128)S(1)} %get-tuple-element.29.product_cols_ref), channel_id=1, source_target_pairs={{16,0},{24,1},{0,2},{8,3},{20,4},{28,5},{4,6},{12,7},{17,8},{25,9}... | collective-permute-start | bytes 393224 | tf_op jit(solution)/shard_map/ppermute | solution.py:87
  16.7 2.8 %shard_map.52.inverse_ref = f32[64,64]{1,0:T(8,128)S(1)} custom-call(f32[64,64]{1,0:T(8,128)S(1)} %get-tuple-element.31.gram_ref), custom_call_target="tpu_custom_call" | custom-call | flops 1073741824 | bytes 262144 | tf_op jit(solution)/shard_map/pallas_call | solution.py:295
  19.5 0.0 collective-permute-done.5.received_ref
  19.5 1.4 %shard_map.53 = (f32[1024,512]{1,0:T(8,128)S(1)}, f32[64,1024]{1,0:T(8,128)}, bf16[192,1024]{1,0:T(8,128)(2,1)S(1)}, f32[64,1024]{1,0:T(8,128)S(1)}, f32[64,512]{1,0:T(8,128)S(1)}, /*index=5*/f32[64,512]{1,0:T(8,128)S(1)}) custom-call(f32[1024,512]{1,0:T(8,128)S(1)} %get-tuple-element.27.matrix_ref, f32[64,1024]{1,0:T(8,128)S(1)} %get-tuple-element.30.panel_ref, ...), custom_call_target="tpu_custom_call" | custom-call | flops 1073741824 | bytes 262144 | tf_op jit(solution)/shard_map/pallas_call | solution.py:295
  20.9 1.9 %collective-permute-done.2.refs_0_ = f32[64,512]{1,0:T(8,128)S(1)} collective-permute-done((f32[64,512]{1,0:T(8,128)S(1)}, f32[64,512]{1,0:T(8,128)S(1)}, u32[]{:S(2)}, u32[]{:S(2)}) %collective-permute-start.2) | collective-permute-done | bytes 131104 | tf_op jit(solution)/shard_map/ppermute | solution.py:87
  22.8 0.4 %shard_map.55.refs_3_ = f32[64,64]{1,0:T(8,128)S(1)} custom-call(f32[64,512]{1,0:T(8,128)S(1)} %collective-permute-done.2.refs_0_, f32[64,512]{1,0:T(8,128)S(1)} %collective-permute-done.3.refs_1_, bf16[192,512]{1,0:T(8,128)(2,1)S(1)} %get-tuple-element.44.refs_2_, bf16[192,512]{1,0:T(8,128)(2,1)S(1)} %get-tuple-element.45.refs_3_), custom_call_target="tpu_custom_call" | custom-call | flops 16777216 | bytes 262144 | tf_op jit(solution)/shard_map/pallas_call | solution.py:295
  23.1 0.9 %collective-permute-start.6 = (f32[64,64]{1,0:T(8,128)S(1)}, f32[64,64]{1,0:T(8,128)S(1)}, u32[]{:S(2)}, u32[]{:S(2)}) collective-permute-start(f32[64,64]{1,0:T(8,128)S(1)} %shard_map.55.refs_3_), channel_id=1, source_target_pairs={{0,24},{8,16},{16,8},{24,0},{1,25},{9,17},{17,9},{25,1},{2,26},{10... | collective-permute-start | bytes 49160 | tf_op jit(solution)/shard_map/ppermute | solution.py:38
  24.0 0.8 %collective-permute-start.7 = (f32[64,64]{1,0:T(8,128)S(1)}, f32[64,64]{1,0:T(8,128)S(1)}, u32[]{:S(2)}, u32[]{:S(2)}) collective-permute-start(f32[64,64]{1,0:T(8,128)S(1)} %shard_map.55.refs_3_), channel_id=1, source_target_pairs={{0,16},{8,24},{16,0},{24,8},{1,17},{9,25},{17,1},{25,9},{2,18},{10... | collective-permute-start | bytes 49160 | tf_op jit(solution)/shard_map/ppermute | solution.py:38
  24.8 0.3 collective-permute-start.8
  25.1 0.8 %shard_map.54 = (f32[1024,512]{1,0:T(8,128)S(1)}, f32[64,1024]{1,0:T(8,128)S(1)}) custom-call(s32[1]{0:T(128)} %bitcast.which_ref, f32[1024,512]{1,0:T(8,128)S(1)} %get-tuple-element.35.begun_ref, f32[64,512]{1,0:T(8,128)S(1)} %get-tuple-element.36.cols_ref, f32[64,64]{1,0:T(8,128)S(1)} %shard_map.52.inverse_ref, ...), custom_call_target="tpu_custom_call" | custom-call | flops 1073741824 | bytes 262144 | tf_op jit(solution)/shard_map/pallas_call | solution.py:295
  25.9 0.9 %collective-permute-done.6.refs_0_ = f32[64,64]{1,0:T(8,128)S(1)} collective-permute-done((f32[64,64]{1,0:T(8,128)S(1)}, f32[64,64]{1,0:T(8,128)S(1)}, u32[]{:S(2)}, u32[]{:S(2)}) %collective-permute-start.6) | collective-permute-done | bytes 16416 | tf_op jit(solution)/shard_map/ppermute | solution.py:38
  26.8 1.2 %collective-permute-done.7.refs_1_ = f32[64,64]{1,0:T(8,128)S(1)} collective-permute-done((f32[64,64]{1,0:T(8,128)S(1)}, f32[64,64]{1,0:T(8,128)S(1)}, u32[]{:S(2)}, u32[]{:S(2)}) %collective-permute-start.7) | collective-permute-done | bytes 16416 | tf_op jit(solution)/shard_map/ppermute | solution.py:38
  28.0 0.0 collective-permute-done.8.refs_2_
  28.0 2.2 %shard_map.56 = (f32[1024,512]{1,0:T(8,128)}, f32[64,1024]{1,0:T(8,128)}) custom-call(f32[1024,512]{1,0:T(8,128)S(1)} %get-tuple-element.39.further_ref, f32[64,1024]{1,0:T(8,128)S(1)} %get-tuple-element.40.image_ref, bf16[192,1024]{1,0:T(8,128)(2,1)S(1)} %get-tuple-element.41.left_ref, f32[64,1024]{1,0:T(8,128)S(1)} %get-tuple-element.42.coeffs_ref, ...), custom_call_target="tpu_custom_call" | custom-call | flops 1073741824 | bytes 262144 | tf_op jit(solution)/shard_map/pallas_call | solution.py:295
  (4 shorter events, 0.0 us)
Async XLA Ops:
  3.3 3.1 %collective-permute-start = (f32[72,512]{1,0:T(8,128)S(1)}, f32[72,512]{1,0:T(8,128)S(1)}, u32[]{:S(2)}, u32[]{:S(2)}) collective-permute-start(f32[72,512]{1,0:T(8,128)S(1)} %shard_map.50), channel_id=1, source_target_pairs={{0,8},{8,0},{16,24},{24,16},{1,9},{9,1},{17,25},{25,17},{2,10},{10... | collective-permute-start | bytes 442376 | tf_op jit(solution)/shard_map/ppermute | solution.py:38
  3.8 4.0 %collective-permute-start.4 = (f32[64,512]{1,0:T(8,128)S(1)}, f32[64,512]{1,0:T(8,128)}, u32[]{:S(2)}, u32[]{:S(2)}) collective-permute-start(f32[64,512]{1,0:T(8,128)S(1)} %get-tuple-element.32), channel_id=1, source_target_pairs={{0,8},{9,1},{18,26},{27,19},{4,12},{13,5},{22,30},{31,23}} | collective-permute-start | bytes 393224 | tf_op jit(solution)/shard_map/ppermute | solution.py:69
  6.4 5.8 %collective-permute-start.1 = (f32[72,512]{1,0:T(8,128)S(1)}, f32[72,512]{1,0:T(8,128)S(1)}, u32[]{:S(2)}, u32[]{:S(2)}) collective-permute-start(f32[72,512]{1,0:T(8,128)S(1)} %add.8.mine_ref), channel_id=1, source_target_pairs={{0,16},{8,24},{16,0},{24,8},{1,17},{9,25},{17,1},{25,9},{2,18},{10... | collective-permute-start | bytes 442376 | tf_op jit(solution)/shard_map/ppermute | solution.py:38
  7.8 11.7 %collective-permute-start.5 = (f32[64,512]{1,0:T(8,128)S(1)}, f32[64,512]{1,0:T(8,128)S(1)}, u32[]{:S(2)}, u32[]{:S(2)}) collective-permute-start(f32[64,512]{1,0:T(8,128)S(1)} %broadcast_select_fusion.held_ref), channel_id=1, source_target_pairs={{0,16},{8,24},{9,25},{1,17},{18,2},{26,10},{27,11},{19,3},{4,20},{... | collective-permute-start | bytes 393224 | tf_op jit(solution)/shard_map/ppermute | solution.py:69
  12.3 10.5 %collective-permute-start.2 = (f32[64,512]{1,0:T(8,128)S(1)}, f32[64,512]{1,0:T(8,128)S(1)}, u32[]{:S(2)}, u32[]{:S(2)}) collective-permute-start(f32[64,512]{1,0:T(8,128)S(1)} %get-tuple-element.29.product_cols_ref), channel_id=1, source_target_pairs={{4,0},{12,1},{20,2},{28,3},{0,4},{8,5},{16,6},{24,7},{5,8},{13,9},... | collective-permute-start | bytes 393224 | tf_op jit(solution)/shard_map/ppermute | solution.py:87
  15.8 7.0 %collective-permute-start.3 = (f32[64,512]{1,0:T(8,128)S(1)}, f32[64,512]{1,0:T(8,128)S(1)}, u32[]{:S(2)}, u32[]{:S(2)}) collective-permute-start(f32[64,512]{1,0:T(8,128)S(1)} %get-tuple-element.29.product_cols_ref), channel_id=1, source_target_pairs={{16,0},{24,1},{0,2},{8,3},{20,4},{28,5},{4,6},{12,7},{17,8},{25,9}... | collective-permute-start | bytes 393224 | tf_op jit(solution)/shard_map/ppermute | solution.py:87
  23.1 3.6 %collective-permute-start.6 = (f32[64,64]{1,0:T(8,128)S(1)}, f32[64,64]{1,0:T(8,128)S(1)}, u32[]{:S(2)}, u32[]{:S(2)}) collective-permute-start(f32[64,64]{1,0:T(8,128)S(1)} %shard_map.55.refs_3_), channel_id=1, source_target_pairs={{0,24},{8,16},{16,8},{24,0},{1,25},{9,17},{17,9},{25,1},{2,26},{10... | collective-permute-start | bytes 49160 | tf_op jit(solution)/shard_map/ppermute | solution.py:38
  24.0 3.9 %collective-permute-start.7 = (f32[64,64]{1,0:T(8,128)S(1)}, f32[64,64]{1,0:T(8,128)S(1)}, u32[]{:S(2)}, u32[]{:S(2)}) collective-permute-start(f32[64,64]{1,0:T(8,128)S(1)} %shard_map.55.refs_3_), channel_id=1, source_target_pairs={{0,16},{8,24},{16,0},{24,8},{1,17},{9,25},{17,1},{25,9},{2,18},{10... | collective-permute-start | bytes 49160 | tf_op jit(solution)/shard_map/ppermute | solution.py:38
  24.8 3.2 %collective-permute-start.8 = (f32[64,64]{1,0:T(8,128)S(1)}, f32[64,64]{1,0:T(8,128)S(1)}, u32[]{:S(2)}, u32[]{:S(2)}) collective-permute-start(f32[64,64]{1,0:T(8,128)S(1)} %shard_map.55.refs_3_), channel_id=1, source_target_pairs={{0,8},{8,0},{16,24},{24,16},{1,9},{9,1},{17,25},{25,17},{2,10},{10... | collective-permute-start | bytes 49160 | tf_op jit(solution)/shard_map/ppermute | solution.py:38

commit v4 on v3

--- a/solution.py
+++ b/solution.py
@@ -11,7 +11,7 @@
 VMEM = pl.BlockSpec(memory_space=pltpu.VMEM)
 SMEM = pl.BlockSpec(memory_space=pltpu.SMEM)
 HBM = pl.BlockSpec(memory_space=pltpu.HBM)
-PARAMS = pltpu.CompilerParams(vmem_limit_bytes=40 * 1024 * 1024)
+PARAMS = pltpu.CompilerParams(vmem_limit_bytes=20 * 1024 * 1024)
 STRIP = 8
 
 
@@ -82,7 +82,7 @@
         for k in range(ratio):
             for q in range(n_row):
                 column = (k + shift) % ratio * n_row + r
-                row = q if shift % 2 else q ^ (n_row // 2)
+                row = q ^ (n_row // 2) if shift % 2 else q
                 pairs.append((row * n_col + column, r * n_col + k * n_row + q))
     return lax.ppermute(value, ("row", "col"), pairs)
 

time: 30.3 us -> 33 us (1.089)
  starting transfers between devices: 13.4 us -> 15.4 us
  waiting for transfers between devices: 5.72 us -> 6.38 us
    ppermute x5, starting transfers between devices: 3.78 us -> 5.5 us  [partner(): return lax.ppermute(value, axis, [(i, i ^ step) for i in range(size)])]
    ppermute x5, waiting for transfers between devices: 3.85 us -> 4.53 us  [partner(): return lax.ppermute(value, axis, [(i, i ^ step) for i in range(size)])]
  transfers between devices with their start and end apart: 9 -> 9, of which waited for: 4 -> 4; matrix products, arithmetic and copies ran while one was open for 0% -> 0% of each run, Pallas kernels for 17% -> 15%
where the time goes in v4:
time: 33 us; the launch traced here: 32.8 us
  starting transfers between devices  15.4 us (47%)
  Pallas kernels  10.2 us (31%)
  waiting for transfers between devices  6.38 us (19%)
  between operations  0.72 us (2%)
    pallas_call x8, Pallas kernels, call(): pl.pallas_call(kernel, out_shape=outs, in_specs=in_specs or [VMEM] * len(...  10.2 us
    ppermute x5, starting transfers between devices, partner(): return lax.ppermute(value, axis, [(i, i ^ step) for i in range(size)])  5.5 us
    ppermute x2, starting transfers between devices, spread_rows(): received = lax.ppermute(value, ('row', 'col'), pairs)  5.28 us
    ppermute x2, starting transfers between devices, transpose_grid(): return lax.ppermute(value, ('row', 'col'), pairs)  4.61 us
    ppermute x5, waiting for transfers between devices, partner(): return lax.ppermute(value, axis, [(i, i ^ step) for i in range(size)])  4.53 us
    ppermute x2, waiting for transfers between devices, transpose_grid(): return lax.ppermute(value, ('row', 'col'), pairs)  1.84 us
  transfers between devices with their start and end apart: 9, of which 4 were waited for; matrix products, arithmetic and copies ran while one was open for 0% of the time, Pallas kernels for 15%

profile of v4, /device:TPU:0, one launch (start us, length us, event | category | flops | bytes accessed | tf_op | source)
XLA Modules:
  0.0 32.8 jit_solution(11121406648945088620)
XLA Ops:
  0.6 1.8 %shard_map.49 = (bf16[192,512]{1,0:T(8,128)(2,1)S(1)}, bf16[192,512]{1,0:T(8,128)(2,1)S(1)}, f32[64,512]{1,0:T(8,128)S(1)}, f32[64,1024]{1,0:T(8,128)S(1)}, bf16...) custom-call(s32[1]{0:T(128)} %bitcast.which_ref, f32[64,1024]{1,0:T(8,128)} %bitcast.5, ...), custom_call_target="tpu_custom_call" | custom-call | flops 268435456 | bytes 262144 | tf_op jit(solution)/shard_map/pallas_call | solution.py:295
  2.5 0.8 %shard_map.50 = f32[72,512]{1,0:T(8,128)S(1)} custom-call(bf16[192,1024]{1,0:T(8,128)(2,1)S(1)} %get-tuple-element.26.terms_ref, f32[1024,512]{1,0:T(8,128)S(1)} %get-tuple-element.27.matrix_ref, f32[8,512]{1,0:T(8,128)S(1)} %get-tuple-element.28.gram_ref), custom_call_target="tpu_custom_call" | custom-call | flops 1073741824 | bytes 262144 | tf_op jit(solution)/shard_map/pallas_call | solution.py:295
  3.3 0.5 %collective-permute-start = (f32[72,512]{1,0:T(8,128)S(1)}, f32[72,512]{1,0:T(8,128)S(1)}, u32[]{:S(2)}, u32[]{:S(2)}) collective-permute-start(f32[72,512]{1,0:T(8,128)S(1)} %shard_map.50), channel_id=1, source_target_pairs={{0,8},{8,0},{16,24},{24,16},{1,9},{9,1},{17,25},{25,17},{2,10},{10... | collective-permute-start | bytes 442376 | tf_op jit(solution)/shard_map/ppermute | solution.py:38
  3.8 2.6 %collective-permute-start.4 = (f32[64,512]{1,0:T(8,128)S(1)}, f32[64,512]{1,0:T(8,128)}, u32[]{:S(2)}, u32[]{:S(2)}) collective-permute-start(f32[64,512]{1,0:T(8,128)S(1)} %get-tuple-element.32), channel_id=1, source_target_pairs={{0,8},{9,1},{18,26},{27,19},{4,12},{13,5},{22,30},{31,23}} | collective-permute-start | bytes 393224 | tf_op jit(solution)/shard_map/ppermute | solution.py:69
  6.4 0.0 collective-permute-done
  6.4 1.3 %collective-permute-start.1 = (f32[72,512]{1,0:T(8,128)S(1)}, f32[72,512]{1,0:T(8,128)S(1)}, u32[]{:S(2)}, u32[]{:S(2)}) collective-permute-start(f32[72,512]{1,0:T(8,128)S(1)} %add.8.mine_ref), channel_id=1, source_target_pairs={{0,16},{8,24},{16,0},{24,8},{1,17},{9,25},{17,1},{25,9},{2,18},{10... | collective-permute-start | bytes 442376 | tf_op jit(solution)/shard_map/ppermute | solution.py:38
  7.8 2.7 %collective-permute-start.5 = (f32[64,512]{1,0:T(8,128)S(1)}, f32[64,512]{1,0:T(8,128)S(1)}, u32[]{:S(2)}, u32[]{:S(2)}) collective-permute-start(f32[64,512]{1,0:T(8,128)S(1)} %broadcast_select_fusion.held_ref), channel_id=1, source_target_pairs={{0,16},{8,24},{9,25},{1,17},{18,2},{26,10},{27,11},{19,3},{4,20},{... | collective-permute-start | bytes 393224 | tf_op jit(solution)/shard_map/ppermute | solution.py:69
  10.5 1.8 %collective-permute-done.1.other_ref = f32[72,512]{1,0:T(8,128)S(1)} collective-permute-done((f32[72,512]{1,0:T(8,128)S(1)}, f32[72,512]{1,0:T(8,128)S(1)}, u32[]{:S(2)}, u32[]{:S(2)}) %collective-permute-start.1) | collective-permute-done | bytes 147488 | tf_op jit(solution)/shard_map/ppermute | solution.py:38
  12.2 0.1 shard_map.51
  12.3 4.0 %collective-permute-start.2 = (f32[64,512]{1,0:T(8,128)S(1)}, f32[64,512]{1,0:T(8,128)S(1)}, u32[]{:S(2)}, u32[]{:S(2)}) collective-permute-start(f32[64,512]{1,0:T(8,128)S(1)} %get-tuple-element.29.product_cols_ref), channel_id=1, source_target_pairs={{20,0},{28,1},{4,2},{12,3},{16,4},{24,5},{0,6},{8,7},{21,8},{29,9}... | collective-permute-start | bytes 393224 | tf_op jit(solution)/shard_map/ppermute | solution.py:87
  16.3 0.7 %collective-permute-start.3 = (f32[64,512]{1,0:T(8,128)S(1)}, f32[64,512]{1,0:T(8,128)S(1)}, u32[]{:S(2)}, u32[]{:S(2)}) collective-permute-start(f32[64,512]{1,0:T(8,128)S(1)} %get-tuple-element.29.product_cols_ref), channel_id=1, source_target_pairs={{0,0},{8,1},{16,2},{24,3},{4,4},{12,5},{20,6},{28,7},{1,8},{9,9},{... | collective-permute-start | bytes 393224 | tf_op jit(solution)/shard_map/ppermute | solution.py:87
  16.9 2.8 %shard_map.52.inverse_ref = f32[64,64]{1,0:T(8,128)S(1)} custom-call(f32[64,64]{1,0:T(8,128)S(1)} %get-tuple-element.31.gram_ref), custom_call_target="tpu_custom_call" | custom-call | flops 1073741824 | bytes 262144 | tf_op jit(solution)/shard_map/pallas_call | solution.py:295
  19.8 0.0 collective-permute-done.5.received_ref
  19.8 1.4 %shard_map.53 = (f32[1024,512]{1,0:T(8,128)S(1)}, f32[64,1024]{1,0:T(8,128)}, bf16[192,1024]{1,0:T(8,128)(2,1)S(1)}, f32[64,1024]{1,0:T(8,128)S(1)}, f32[64,512]{1,0:T(8,128)S(1)}, /*index=5*/f32[64,512]{1,0:T(8,128)S(1)}) custom-call(f32[1024,512]{1,0:T(8,128)S(1)} %get-tuple-element.27.matrix_ref, f32[64,1024]{1,0:T(8,128)S(1)} %get-tuple-element.30.panel_ref, ...), custom_call_target="tpu_custom_call" | custom-call | flops 1073741824 | bytes 262144 | tf_op jit(solution)/shard_map/pallas_call | solution.py:295
  21.2 1.8 %collective-permute-done.2.refs_0_ = f32[64,512]{1,0:T(8,128)S(1)} collective-permute-done((f32[64,512]{1,0:T(8,128)S(1)}, f32[64,512]{1,0:T(8,128)S(1)}, u32[]{:S(2)}, u32[]{:S(2)}) %collective-permute-start.2) | collective-permute-done | bytes 131104 | tf_op jit(solution)/shard_map/ppermute | solution.py:87
  23.0 0.0 collective-permute-done.3.refs_1_
  23.0 0.3 %shard_map.55.refs_3_ = f32[64,64]{1,0:T(8,128)S(1)} custom-call(f32[64,512]{1,0:T(8,128)S(1)} %collective-permute-done.2.refs_0_, f32[64,512]{1,0:T(8,128)S(1)} %collective-permute-done.3.refs_1_, bf16[192,512]{1,0:T(8,128)(2,1)S(1)} %get-tuple-element.44.refs_2_, bf16[192,512]{1,0:T(8,128)(2,1)S(1)} %get-tuple-element.45.refs_3_), custom_call_target="tpu_custom_call" | custom-call | flops 16777216 | bytes 262144 | tf_op jit(solution)/shard_map/pallas_call | solution.py:295
  23.4 3.3 %collective-permute-start.6 = (f32[64,64]{1,0:T(8,128)S(1)}, f32[64,64]{1,0:T(8,128)S(1)}, u32[]{:S(2)}, u32[]{:S(2)}) collective-permute-start(f32[64,64]{1,0:T(8,128)S(1)} %shard_map.55.refs_3_), channel_id=1, source_target_pairs={{0,24},{8,16},{16,8},{24,0},{1,25},{9,17},{17,9},{25,1},{2,26},{10... | collective-permute-start | bytes 49160 | tf_op jit(solution)/shard_map/ppermute | solution.py:38
  26.6 0.3 %collective-permute-start.7 = (f32[64,64]{1,0:T(8,128)S(1)}, f32[64,64]{1,0:T(8,128)S(1)}, u32[]{:S(2)}, u32[]{:S(2)}) collective-permute-start(f32[64,64]{1,0:T(8,128)S(1)} %shard_map.55.refs_3_), channel_id=1, source_target_pairs={{0,16},{8,24},{16,0},{24,8},{1,17},{9,25},{17,1},{25,9},{2,18},{10... | collective-permute-start | bytes 49160 | tf_op jit(solution)/shard_map/ppermute | solution.py:38
  27.0 0.0 collective-permute-start.8
  27.0 0.8 %shard_map.54 = (f32[1024,512]{1,0:T(8,128)S(1)}, f32[64,1024]{1,0:T(8,128)S(1)}) custom-call(s32[1]{0:T(128)} %bitcast.which_ref, f32[1024,512]{1,0:T(8,128)S(1)} %get-tuple-element.35.begun_ref, f32[64,512]{1,0:T(8,128)S(1)} %get-tuple-element.36.cols_ref, f32[64,64]{1,0:T(8,128)S(1)} %shard_map.52.inverse_ref, ...), custom_call_target="tpu_custom_call" | custom-call | flops 1073741824 | bytes 262144 | tf_op jit(solution)/shard_map/pallas_call | solution.py:295
  27.8 0.6 %collective-permute-done.6.refs_0_ = f32[64,64]{1,0:T(8,128)S(1)} collective-permute-done((f32[64,64]{1,0:T(8,128)S(1)}, f32[64,64]{1,0:T(8,128)S(1)}, u32[]{:S(2)}, u32[]{:S(2)}) %collective-permute-start.6) | collective-permute-done | bytes 16416 | tf_op jit(solution)/shard_map/ppermute | solution.py:38
  28.4 2.1 %collective-permute-done.7.refs_1_ = f32[64,64]{1,0:T(8,128)S(1)} collective-permute-done((f32[64,64]{1,0:T(8,128)S(1)}, f32[64,64]{1,0:T(8,128)S(1)}, u32[]{:S(2)}, u32[]{:S(2)}) %collective-permute-start.7) | collective-permute-done | bytes 16416 | tf_op jit(solution)/shard_map/ppermute | solution.py:38
  30.6 2.2 %shard_map.56 = (f32[1024,512]{1,0:T(8,128)}, f32[64,1024]{1,0:T(8,128)}) custom-call(f32[1024,512]{1,0:T(8,128)S(1)} %get-tuple-element.39.further_ref, f32[64,1024]{1,0:T(8,128)S(1)} %get-tuple-element.40.image_ref, bf16[192,1024]{1,0:T(8,128)(2,1)S(1)} %get-tuple-element.41.left_ref, f32[64,1024]{1,0:T(8,128)S(1)} %get-tuple-element.42.coeffs_ref, ...), custom_call_target="tpu_custom_call" | custom-call | flops 1073741824 | bytes 262144 | tf_op jit(solution)/shard_map/pallas_call | solution.py:295
  (4 shorter events, 0.0 us)
Async XLA Ops:
  3.3 3.1 %collective-permute-start = (f32[72,512]{1,0:T(8,128)S(1)}, f32[72,512]{1,0:T(8,128)S(1)}, u32[]{:S(2)}, u32[]{:S(2)}) collective-permute-start(f32[72,512]{1,0:T(8,128)S(1)} %shard_map.50), channel_id=1, source_target_pairs={{0,8},{8,0},{16,24},{24,16},{1,9},{9,1},{17,25},{25,17},{2,10},{10... | collective-permute-start | bytes 442376 | tf_op jit(solution)/shard_map/ppermute | solution.py:38
  3.8 4.0 %collective-permute-start.4 = (f32[64,512]{1,0:T(8,128)S(1)}, f32[64,512]{1,0:T(8,128)}, u32[]{:S(2)}, u32[]{:S(2)}) collective-permute-start(f32[64,512]{1,0:T(8,128)S(1)} %get-tuple-element.32), channel_id=1, source_target_pairs={{0,8},{9,1},{18,26},{27,19},{4,12},{13,5},{22,30},{31,23}} | collective-permute-start | bytes 393224 | tf_op jit(solution)/shard_map/ppermute | solution.py:69
  6.4 5.8 %collective-permute-start.1 = (f32[72,512]{1,0:T(8,128)S(1)}, f32[72,512]{1,0:T(8,128)S(1)}, u32[]{:S(2)}, u32[]{:S(2)}) collective-permute-start(f32[72,512]{1,0:T(8,128)S(1)} %add.8.mine_ref), channel_id=1, source_target_pairs={{0,16},{8,24},{16,0},{24,8},{1,17},{9,25},{17,1},{25,9},{2,18},{10... | collective-permute-start | bytes 442376 | tf_op jit(solution)/shard_map/ppermute | solution.py:38
  7.8 12.0 %collective-permute-start.5 = (f32[64,512]{1,0:T(8,128)S(1)}, f32[64,512]{1,0:T(8,128)S(1)}, u32[]{:S(2)}, u32[]{:S(2)}) collective-permute-start(f32[64,512]{1,0:T(8,128)S(1)} %broadcast_select_fusion.held_ref), channel_id=1, source_target_pairs={{0,16},{8,24},{9,25},{1,17},{18,2},{26,10},{27,11},{19,3},{4,20},{... | collective-permute-start | bytes 393224 | tf_op jit(solution)/shard_map/ppermute | solution.py:69
  12.3 10.7 %collective-permute-start.2 = (f32[64,512]{1,0:T(8,128)S(1)}, f32[64,512]{1,0:T(8,128)S(1)}, u32[]{:S(2)}, u32[]{:S(2)}) collective-permute-start(f32[64,512]{1,0:T(8,128)S(1)} %get-tuple-element.29.product_cols_ref), channel_id=1, source_target_pairs={{20,0},{28,1},{4,2},{12,3},{16,4},{24,5},{0,6},{8,7},{21,8},{29,9}... | collective-permute-start | bytes 393224 | tf_op jit(solution)/shard_map/ppermute | solution.py:87
  16.3 6.7 %collective-permute-start.3 = (f32[64,512]{1,0:T(8,128)S(1)}, f32[64,512]{1,0:T(8,128)S(1)}, u32[]{:S(2)}, u32[]{:S(2)}) collective-permute-start(f32[64,512]{1,0:T(8,128)S(1)} %get-tuple-element.29.product_cols_ref), channel_id=1, source_target_pairs={{0,0},{8,1},{16,2},{24,3},{4,4},{12,5},{20,6},{28,7},{1,8},{9,9},{... | collective-permute-start | bytes 393224 | tf_op jit(solution)/shard_map/ppermute | solution.py:87
  23.4 5.1 %collective-permute-start.6 = (f32[64,64]{1,0:T(8,128)S(1)}, f32[64,64]{1,0:T(8,128)S(1)}, u32[]{:S(2)}, u32[]{:S(2)}) collective-permute-start(f32[64,64]{1,0:T(8,128)S(1)} %shard_map.55.refs_3_), channel_id=1, source_target_pairs={{0,24},{8,16},{16,8},{24,0},{1,25},{9,17},{17,9},{25,1},{2,26},{10... | collective-permute-start | bytes 49160 | tf_op jit(solution)/shard_map/ppermute | solution.py:38
  26.6 3.9 %collective-permute-start.7 = (f32[64,64]{1,0:T(8,128)S(1)}, f32[64,64]{1,0:T(8,128)S(1)}, u32[]{:S(2)}, u32[]{:S(2)}) collective-permute-start(f32[64,64]{1,0:T(8,128)S(1)} %shard_map.55.refs_3_), channel_id=1, source_target_pairs={{0,16},{8,24},{16,0},{24,8},{1,17},{9,25},{17,1},{25,9},{2,18},{10... | collective-permute-start | bytes 49160 | tf_op jit(solution)/shard_map/ppermute | solution.py:38
  27.0 3.6 %collective-permute-start.8 = (f32[64,64]{1,0:T(8,128)S(1)}, f32[64,64]{1,0:T(8,128)S(1)}, u32[]{:S(2)}, u32[]{:S(2)}) collective-permute-start(f32[64,64]{1,0:T(8,128)S(1)} %shard_map.55.refs_3_), channel_id=1, source_target_pairs={{0,8},{8,0},{16,24},{24,16},{1,9},{9,1},{17,25},{25,17},{2,10},{10... | collective-permute-start | bytes 49160 | tf_op jit(solution)/shard_map/ppermute | solution.py:38

commit v5 on v1

--- a/solution.py
+++ b/solution.py
@@ -36,6 +36,22 @@
 def partner(value, axis, step):
     size = lax.axis_size(axis)
     return lax.ppermute(value, axis, [(i, i ^ step) for i in range(size)])
+
+
+def tree_sum(parts):
+    while len(parts) > 1:
+        parts = [parts[i] + parts[i + 1] for i in range(0, len(parts), 2)]
+    return parts[0]
+
+
+def group_parts(value, axis, low, high):
+    parts = [value]
+    while low < high:
+        value = tree_sum(parts)
+        radix = min(4, high // low)
+        parts = [value] + [partner(value, axis, i * low) for i in range(1, radix)]
+        low *= radix
+    return parts
 
 
 def spread_rows(value, after):
@@ -183,18 +199,14 @@
 
 
 def basis_kernel(
-    matrix_ref, panel_ref, product_cols_ref, inverse_ref, received_ref, held_ref, takes_ref,
-    begun_ref, basis_ref, left_ref, coeffs_ref, cols_ref, coeffs_cols_ref,
+    matrix_ref, panel_ref, product_cols_ref, inverse_ref,
+    begun_ref, basis_ref, left_ref, coeffs_ref,
 ):
     inverse = inverse_ref[...]
     basis = dot(inverse, panel_ref[...], ((1,), (0,)))
     image_cols = dot(inverse, product_cols_ref[...], ((1,), (0,)))
     basis_ref[...] = basis
     coeffs_ref[...] = dot(inverse, basis, ((0,), (0,)))
-    panel_cols = jnp.where(takes_ref[0] != 0, received_ref[...], held_ref[...])
-    cols = dot(inverse, panel_cols, ((1,), (0,)))
-    cols_ref[...] = cols
-    coeffs_cols_ref[...] = dot(inverse, cols, ((0,), (0,)))
     left = stack_left(basis)
     left_ref[...] = left
     right = stack_right(2.0 * image_cols)
@@ -202,6 +214,14 @@
     for start in range(0, matrix_ref.shape[0], chunk):
         span = slice(start, start + chunk)
         begun_ref[span, :] = matrix_ref[span, :] - dot16(left[:, span], right, ((0,), (0,)))
+
+
+def columns_kernel(inverse_ref, received_ref, held_ref, takes_ref, cols_ref, coeffs_cols_ref):
+    inverse = inverse_ref[...]
+    panel_cols = jnp.where(takes_ref[0] != 0, received_ref[...], held_ref[...])
+    cols = dot(inverse, panel_cols, ((1,), (0,)))
+    cols_ref[...] = cols
+    coeffs_cols_ref[...] = dot(inverse, cols, ((0,), (0,)))
 
 
 def inner_kernel(*refs):
@@ -235,11 +255,11 @@
 
 
 def update_kernel(
-    further_ref, image_ref, left_ref, coeffs_ref, coeffs_cols_ref, inverse_ref,
-    inner_ref, other_ref, updated_ref, w_ref, buffer_ref, w_buffer_ref, sems,
+    further_ref, image_ref, left_ref, coeffs_ref, coeffs_cols_ref, inverse_ref, *refs
 ):
+    inners, (updated_ref, w_ref, buffer_ref, w_buffer_ref, sems) = refs[:-5], refs[-5:]
     inverse = inverse_ref[...]
-    inner = inner_ref[...] + other_ref[...]
+    inner = tree_sum([part[...] for part in inners])
     right = dot(inverse, dot(inner, coeffs_cols_ref[...], ((1,), (0,))), ((1,), (0,)))
     right = stack_right(4.0 * right)
     count = sems.shape[0] - 1
@@ -310,28 +330,33 @@
         message = message + partner(message, "row", step)
         step *= 2
     last = partner(message, "row", step)
-    held, received, takes = spread_rows(mines[0], message)
     product_cols, gram = call(
         finish_kernel, (shape(width, cols), shape(width, width)), (last, message), flops=1 << 24
     )
     halves = [transpose_grid(product_cols, shift) for shift in reversed(range(ratio))]
+    held, received, takes = spread_rows(mines[0], product_cols)
     inverse = call(factor_kernel, shape(width, width), (gram,), flops=1 << 30)
-    begun, basis, left, coeffs, basis_cols, coeffs_cols = call(
+    begun, basis, left, coeffs = call(
         basis_kernel,
         (
             shape(rows, cols),
             shape(width, rows),
             shape(3 * width, rows, dtype=jnp.bfloat16),
             shape(width, rows),
-            shape(width, cols),
-            shape(width, cols),
         ),
-        (kept, panel_t, product_cols, inverse, received, held, takes),
-        in_specs=[VMEM] * 6 + [SMEM],
+        (kept, panel_t, product_cols, inverse),
         flops=1 << 30,
     )
     halves, begun = lax.optimization_barrier((halves, begun))
     inner = call(inner_kernel, shape(width, width), (*halves, *mines[::-1]), flops=1 << 24)
+    received, _ = lax.optimization_barrier((received, inner))
+    basis_cols, coeffs_cols = call(
+        columns_kernel,
+        (shape(width, cols), shape(width, cols)),
+        (inverse, received, held, takes),
+        in_specs=[VMEM] * 3 + [SMEM],
+        flops=1 << 24,
+    )
     further, image = call(
         functools.partial(image_kernel, ratio),
         (shape(rows, cols), shape(width, rows)),
@@ -339,17 +364,11 @@
         in_specs=[SMEM] + [VMEM] * (3 + ratio),
         flops=1 << 30,
     )
-    step = 1
-    while 2 * step < n_row:
-        inner = inner + partner(inner, "row", step)
-        step *= 2
+    inners = group_parts(inner, "row", 1, n_row)[::-1]
     updated, w_rows = call(
         update_kernel,
         (shape(rows, cols), shape(width, rows)),
-        (
-            further, image, left, coeffs, coeffs_cols, inverse,
-            inner, partner(inner, "row", step),
-        ),
+        (further, image, left, coeffs, coeffs_cols, inverse, *inners),
         out_specs=(HBM, HBM),
         scratch=[
             pltpu.VMEM((rows, cols), jnp.float32),

time: 30.5 us -> 30.6 us (level)
  waiting for transfers between devices: 4.65 us -> 4.32 us
    ppermute x2, starting transfers between devices: 4.01 us -> 4.64 us  [spread_rows(): received = lax.ppermute(value, ('row', 'col'), pairs)]
    ppermute x2, starting transfers between devices: 4.91 us -> 4.33 us  [transpose_grid(): return lax.ppermute(value, ('row', 'col'), pairs)]
    ppermute x4 -> x5, waiting for transfers between devices: 4.63 us -> 4.31 us  [partner(): return lax.ppermute(value, axis, [(i, i ^ step) for i in range(size)])]
    ppermute x4 -> x5, starting transfers between devices: 5.68 us -> 5.92 us  [partner(): return lax.ppermute(value, axis, [(i, i ^ step) for i in range(size)])]
    pallas_call x8 -> x9, Pallas kernels: 10.2 us -> 10.5 us  [call(): pl.pallas_call(kernel, out_shape=outs, in_specs=in_specs or [VMEM] * len(...]
  transfers between devices with their start and end apart: 8 -> 9, of which waited for: 3 -> 3; matrix products, arithmetic and copies ran while one was open for 0% -> 0% of each run, Pallas kernels for 17% -> 19%
where the time goes in v5:
time: 30.6 us; the launch traced here: 30.5 us
  starting transfers between devices  14.9 us (49%)
  Pallas kernels  10.5 us (34%)
  waiting for transfers between devices  4.32 us (14%)
  between operations  0.75 us (2%)
    pallas_call x9, Pallas kernels, call(): pl.pallas_call(kernel, out_shape=outs, in_specs=in_specs or [VMEM] * len(...  10.5 us
    ppermute x5, starting transfers between devices, partner(): return lax.ppermute(value, axis, [(i, i ^ step) for i in range(size)])  5.92 us
    ppermute x2, starting transfers between devices, spread_rows(): received = lax.ppermute(value, ('row', 'col'), pairs)  4.64 us
    ppermute x2, starting transfers between devices, transpose_grid(): return lax.ppermute(value, ('row', 'col'), pairs)  4.33 us
    ppermute x5, waiting for transfers between devices, partner(): return lax.ppermute(value, axis, [(i, i ^ step) for i in range(size)])  4.31 us
  transfers between devices with their start and end apart: 9, of which 3 were waited for; matrix products, arithmetic and copies ran while one was open for 0% of the time, Pallas kernels for 19%

profile of v5, /device:TPU:0, one launch (start us, length us, event | category | flops | bytes accessed | tf_op | source)
XLA Modules:
  0.0 30.5 jit_solution(10392269652534521116)
XLA Ops:
  0.6 1.8 %shard_map.49 = (f32[64,512]{1,0:T(8,128)S(1)}, f32[64,512]{1,0:T(8,128)S(1)}, f32[64,1024]{1,0:T(8,128)S(1)}, bf16[192,1024]{1,0:T(8,128)(2,1)S(1)}, f32[8,512]{1,0:T(8,128)S(1)}, /*index=5*/f32[1024,512]{1,0:T(8,128)S(1)}) custom-call(s32[1]{0:T(128)} %bitcast.which_ref, f32[64,1024]{1,0:T(8,128)} %bitcast.5, f32[1024,512]{1,0:T(8,128)} %matrix_ref.1), custom_call_target="tpu_custom_call" | custom-call | flops 268435456 | bytes 262144 | tf_op jit(solution)/shard_map/pallas_call | solution.py:288
  2.5 0.8 %shard_map.50 = f32[72,512]{1,0:T(8,128)S(1)} custom-call(bf16[192,1024]{1,0:T(8,128)(2,1)S(1)} %get-tuple-element.26.terms_ref, f32[1024,512]{1,0:T(8,128)S(1)} %get-tuple-element.27.matrix_ref, f32[8,512]{1,0:T(8,128)S(1)} %get-tuple-element.28.gram_ref), custom_call_target="tpu_custom_call" | custom-call | flops 1073741824 | bytes 262144 | tf_op jit(solution)/shard_map/pallas_call | solution.py:288
  3.3 0.5 %collective-permute-start = (f32[72,512]{1,0:T(8,128)S(1)}, f32[72,512]{1,0:T(8,128)S(1)}, u32[]{:S(2)}, u32[]{:S(2)}) collective-permute-start(f32[72,512]{1,0:T(8,128)S(1)} %shard_map.50), channel_id=1, source_target_pairs={{0,8},{8,0},{16,24},{24,16},{1,9},{9,1},{17,25},{25,17},{2,10},{10... | collective-permute-start | bytes 442376 | tf_op jit(solution)/shard_map/ppermute | solution.py:38
  3.8 1.0 %collective-permute-done = f32[72,512]{1,0:T(8,128)S(1)} collective-permute-done((f32[72,512]{1,0:T(8,128)S(1)}, f32[72,512]{1,0:T(8,128)S(1)}, u32[]{:S(2)}, u32[]{:S(2)}) %collective-permute-start) | collective-permute-done | bytes 147488 | tf_op jit(solution)/shard_map/ppermute | solution.py:38
  4.8 2.9 %collective-permute-start.1 = (f32[72,512]{1,0:T(8,128)S(1)}, f32[72,512]{1,0:T(8,128)S(1)}, u32[]{:S(2)}, u32[]{:S(2)}) collective-permute-start(f32[72,512]{1,0:T(8,128)S(1)} %add.8.mine_ref), channel_id=1, source_target_pairs={{0,16},{8,24},{16,0},{24,8},{1,17},{9,25},{17,1},{25,9},{2,18},{10... | collective-permute-start | bytes 442376 | tf_op jit(solution)/shard_map/ppermute | solution.py:38
  7.8 1.8 %collective-permute-start.4 = (f32[64,512]{1,0:T(8,128)S(1)}, f32[64,512]{1,0:T(8,128)S(1)}, u32[]{:S(2)}, u32[]{:S(2)}) collective-permute-start(f32[64,512]{1,0:T(8,128)S(1)} %get-tuple-element.34.refs_3_), channel_id=1, source_target_pairs={{0,8},{9,1},{18,26},{27,19},{4,12},{13,5},{22,30},{31,23}} | collective-permute-start | bytes 393224 | tf_op jit(solution)/shard_map/ppermute | solution.py:69
  9.5 2.4 %collective-permute-done.1.other_ref = f32[72,512]{1,0:T(8,128)S(1)} collective-permute-done((f32[72,512]{1,0:T(8,128)S(1)}, f32[72,512]{1,0:T(8,128)S(1)}, u32[]{:S(2)}, u32[]{:S(2)}) %collective-permute-start.1) | collective-permute-done | bytes 147488 | tf_op jit(solution)/shard_map/ppermute | solution.py:38
  11.9 0.1 shard_map.51
  12.0 2.8 %collective-permute-start.2 = (f32[64,512]{1,0:T(8,128)S(1)}, f32[64,512]{1,0:T(8,128)S(1)}, u32[]{:S(2)}, u32[]{:S(2)}) collective-permute-start(f32[64,512]{1,0:T(8,128)S(1)} %get-tuple-element.29.product_cols_ref), channel_id=1, source_target_pairs={{4,0},{12,1},{20,2},{28,3},{0,4},{8,5},{16,6},{24,7},{5,8},{13,9},... | collective-permute-start | bytes 393224 | tf_op jit(solution)/shard_map/ppermute | solution.py:87
  14.8 1.5 %collective-permute-start.3 = (f32[64,512]{1,0:T(8,128)S(1)}, f32[64,512]{1,0:T(8,128)S(1)}, u32[]{:S(2)}, u32[]{:S(2)}) collective-permute-start(f32[64,512]{1,0:T(8,128)S(1)} %get-tuple-element.29.product_cols_ref), channel_id=1, source_target_pairs={{16,0},{24,1},{0,2},{8,3},{20,4},{28,5},{4,6},{12,7},{17,8},{25,9}... | collective-permute-start | bytes 393224 | tf_op jit(solution)/shard_map/ppermute | solution.py:87
  16.4 2.9 %collective-permute-start.5 = (f32[64,512]{1,0:T(8,128)S(1)}, f32[64,512]{1,0:T(8,128)S(1)}, u32[]{:S(2)}, u32[]{:S(2)}) collective-permute-start(f32[64,512]{1,0:T(8,128)S(1)} %broadcast_select_fusion.held_ref), channel_id=1, source_target_pairs={{0,16},{8,24},{9,25},{1,17},{18,2},{26,10},{27,11},{19,3},{4,20},{... | collective-permute-start | bytes 393224 | tf_op jit(solution)/shard_map/ppermute | solution.py:69
  19.2 2.8 %shard_map.52.inverse_ref = f32[64,64]{1,0:T(8,128)S(1)} custom-call(f32[64,64]{1,0:T(8,128)S(1)} %get-tuple-element.31.gram_ref), custom_call_target="tpu_custom_call" | custom-call | flops 1073741824 | bytes 262144 | tf_op jit(solution)/shard_map/pallas_call | solution.py:288
  22.1 1.1 %shard_map.53 = (f32[1024,512]{1,0:T(8,128)S(1)}, f32[64,1024]{1,0:T(8,128)}, bf16[192,1024]{1,0:T(8,128)(2,1)S(1)}, f32[64,1024]{1,0:T(8,128)S(1)}) custom-call(f32[1024,512]{1,0:T(8,128)S(1)} %get-tuple-element.27.matrix_ref, f32[64,1024]{1,0:T(8,128)S(1)} %get-tuple-element.30.panel_ref, f32[64,512]{1,0:T(8,128)S(1)} %get-tuple-element.29.product_cols_ref, ...), custom_call_target="tpu_custom_call" | custom-call | flops 1073741824 | bytes 262144 | tf_op jit(solution)/shard_map/pallas_call | solution.py:288
  23.2 0.0 collective-permute-done.2.refs_0_
  23.2 0.0 collective-permute-done.3.refs_1_
  23.2 0.4 %shard_map.54.refs_3_ = f32[64,64]{1,0:T(8,128)S(1)} custom-call(f32[64,512]{1,0:T(8,128)S(1)} %collective-permute-done.2.refs_0_, f32[64,512]{1,0:T(8,128)S(1)} %collective-permute-done.3.refs_1_, f32[64,512]{1,0:T(8,128)S(1)} %get-tuple-element.38.refs_2_, f32[64,512]{1,0:T(8,128)S(1)} %get-tuple-element.34.refs_3_), custom_call_target="tpu_custom_call" | custom-call | flops 16777216 | bytes 262144 | tf_op jit(solution)/shard_map/pallas_call | solution.py:288
  23.6 0.1 collective-permute-start.6
  23.7 2.4 %collective-permute-start.7 = (f32[64,64]{1,0:T(8,128)S(1)}, f32[64,64]{1,0:T(8,128)S(1)}, u32[]{:S(2)}, u32[]{:S(2)}) collective-permute-start(f32[64,64]{1,0:T(8,128)S(1)} %shard_map.54.refs_3_), channel_id=1, source_target_pairs={{0,16},{8,24},{16,0},{24,8},{1,17},{9,25},{17,1},{25,9},{2,18},{10... | collective-permute-start | bytes 49160 | tf_op jit(solution)/shard_map/ppermute | solution.py:38
  26.0 0.0 collective-permute-start.8
  26.0 0.0 collective-permute-done.5.received_ref
  26.0 0.5 %shard_map.55 = (f32[64,512]{1,0:T(8,128)S(1)}, f32[64,512]{1,0:T(8,128)S(1)}) custom-call(f32[64,64]{1,0:T(8,128)S(1)} %shard_map.52.inverse_ref, f32[64,512]{1,0:T(8,128)S(1)} %collective-permute-done.5.received_ref, f32[64,512]{1,0:T(8,128)S(1)} %broadcast_select_fusion.held_ref, s32[1]{0:T(128)} %bitcast.2.takes_ref), custom_call_target="tpu_custom_call" | custom-call | flops 16777216 | bytes 262144 | tf_op jit(solution)/shard_map/pallas_call | solution.py:288
  26.5 0.8 %shard_map.56 = (f32[1024,512]{1,0:T(8,128)S(1)}, f32[64,1024]{1,0:T(8,128)S(1)}) custom-call(s32[1]{0:T(128)} %bitcast.which_ref, f32[1024,512]{1,0:T(8,128)S(1)} %get-tuple-element.33.begun_ref, f32[64,512]{1,0:T(8,128)S(1)} %get-tuple-element.40.cols_ref, f32[64,64]{1,0:T(8,128)S(1)} %shard_map.52.inverse_ref, ...), custom_call_target="tpu_custom_call" | custom-call | flops 1073741824 | bytes 262144 | tf_op jit(solution)/shard_map/pallas_call | solution.py:288
  27.3 0.9 %collective-permute-done.7.refs_1_ = f32[64,64]{1,0:T(8,128)S(1)} collective-permute-done((f32[64,64]{1,0:T(8,128)S(1)}, f32[64,64]{1,0:T(8,128)S(1)}, u32[]{:S(2)}, u32[]{:S(2)}) %collective-permute-start.7) | collective-permute-done | bytes 16416 | tf_op jit(solution)/shard_map/ppermute | solution.py:38
  28.3 2.2 %shard_map.57 = (f32[1024,512]{1,0:T(8,128)}, f32[64,1024]{1,0:T(8,128)}) custom-call(f32[1024,512]{1,0:T(8,128)S(1)} %get-tuple-element.41.further_ref, f32[64,1024]{1,0:T(8,128)S(1)} %get-tuple-element.42.image_ref, bf16[192,1024]{1,0:T(8,128)(2,1)S(1)} %get-tuple-element.43.left_ref, f32[64,1024]{1,0:T(8,128)S(1)} %get-tuple-element.44.coeffs_ref, ...), custom_call_target="tpu_custom_call" | custom-call | flops 1073741824 | bytes 262144 | tf_op jit(solution)/shard_map/pallas_call | solution.py:288
  (5 shorter events, 0.0 us)
Async XLA Ops:
  3.3 1.5 %collective-permute-start = (f32[72,512]{1,0:T(8,128)S(1)}, f32[72,512]{1,0:T(8,128)S(1)}, u32[]{:S(2)}, u32[]{:S(2)}) collective-permute-start(f32[72,512]{1,0:T(8,128)S(1)} %shard_map.50), channel_id=1, source_target_pairs={{0,8},{8,0},{16,24},{24,16},{1,9},{9,1},{17,25},{25,17},{2,10},{10... | collective-permute-start | bytes 442376 | tf_op jit(solution)/shard_map/ppermute | solution.py:38
  4.8 7.1 %collective-permute-start.1 = (f32[72,512]{1,0:T(8,128)S(1)}, f32[72,512]{1,0:T(8,128)S(1)}, u32[]{:S(2)}, u32[]{:S(2)}) collective-permute-start(f32[72,512]{1,0:T(8,128)S(1)} %add.8.mine_ref), channel_id=1, source_target_pairs={{0,16},{8,24},{16,0},{24,8},{1,17},{9,25},{17,1},{25,9},{2,18},{10... | collective-permute-start | bytes 442376 | tf_op jit(solution)/shard_map/ppermute | solution.py:38
  7.8 8.6 %collective-permute-start.4 = (f32[64,512]{1,0:T(8,128)S(1)}, f32[64,512]{1,0:T(8,128)S(1)}, u32[]{:S(2)}, u32[]{:S(2)}) collective-permute-start(f32[64,512]{1,0:T(8,128)S(1)} %get-tuple-element.34.refs_3_), channel_id=1, source_target_pairs={{0,8},{9,1},{18,26},{27,19},{4,12},{13,5},{22,30},{31,23}} | collective-permute-start | bytes 393224 | tf_op jit(solution)/shard_map/ppermute | solution.py:69
  12.0 11.2 %collective-permute-start.2 = (f32[64,512]{1,0:T(8,128)S(1)}, f32[64,512]{1,0:T(8,128)S(1)}, u32[]{:S(2)}, u32[]{:S(2)}) collective-permute-start(f32[64,512]{1,0:T(8,128)S(1)} %get-tuple-element.29.product_cols_ref), channel_id=1, source_target_pairs={{4,0},{12,1},{20,2},{28,3},{0,4},{8,5},{16,6},{24,7},{5,8},{13,9},... | collective-permute-start | bytes 393224 | tf_op jit(solution)/shard_map/ppermute | solution.py:87
  14.8 8.4 %collective-permute-start.3 = (f32[64,512]{1,0:T(8,128)S(1)}, f32[64,512]{1,0:T(8,128)S(1)}, u32[]{:S(2)}, u32[]{:S(2)}) collective-permute-start(f32[64,512]{1,0:T(8,128)S(1)} %get-tuple-element.29.product_cols_ref), channel_id=1, source_target_pairs={{16,0},{24,1},{0,2},{8,3},{20,4},{28,5},{4,6},{12,7},{17,8},{25,9}... | collective-permute-start | bytes 393224 | tf_op jit(solution)/shard_map/ppermute | solution.py:87
  16.4 9.7 %collective-permute-start.5 = (f32[64,512]{1,0:T(8,128)S(1)}, f32[64,512]{1,0:T(8,128)S(1)}, u32[]{:S(2)}, u32[]{:S(2)}) collective-permute-start(f32[64,512]{1,0:T(8,128)S(1)} %broadcast_select_fusion.held_ref), channel_id=1, source_target_pairs={{0,16},{8,24},{9,25},{1,17},{18,2},{26,10},{27,11},{19,3},{4,20},{... | collective-permute-start | bytes 393224 | tf_op jit(solution)/shard_map/ppermute | solution.py:69
  23.6 3.8 %collective-permute-start.6 = (f32[64,64]{1,0:T(8,128)S(1)}, f32[64,64]{1,0:T(8,128)S(1)}, u32[]{:S(2)}, u32[]{:S(2)}) collective-permute-start(f32[64,64]{1,0:T(8,128)S(1)} %shard_map.54.refs_3_), channel_id=1, source_target_pairs={{0,24},{8,16},{16,8},{24,0},{1,25},{9,17},{17,9},{25,1},{2,26},{10... | collective-permute-start | bytes 49160 | tf_op jit(solution)/shard_map/ppermute | solution.py:38
  23.7 4.6 %collective-permute-start.7 = (f32[64,64]{1,0:T(8,128)S(1)}, f32[64,64]{1,0:T(8,128)S(1)}, u32[]{:S(2)}, u32[]{:S(2)}) collective-permute-start(f32[64,64]{1,0:T(8,128)S(1)} %shard_map.54.refs_3_), channel_id=1, source_target_pairs={{0,16},{8,24},{16,0},{24,8},{1,17},{9,25},{17,1},{25,9},{2,18},{10... | collective-permute-start | bytes 49160 | tf_op jit(solution)/shard_map/ppermute | solution.py:38
  26.0 2.2 %collective-permute-start.8 = (f32[64,64]{1,0:T(8,128)S(1)}, f32[64,64]{1,0:T(8,128)S(1)}, u32[]{:S(2)}, u32[]{:S(2)}) collective-permute-start(f32[64,64]{1,0:T(8,128)S(1)} %shard_map.54.refs_3_), channel_id=1, source_target_pairs={{0,8},{8,0},{16,24},{24,16},{1,9},{9,1},{17,25},{25,17},{2,10},{10... | collective-permute-start | bytes 49160 | tf_op jit(solution)/shard_map/ppermute | solution.py:38
